TPU v7x, 32 devices: a whole 2x2x4 slice. The times are simulated.
32 devices in a mesh: seq: 8 (over z, y), wt: 4 (over x, core).
Axes of the slice: x: 2, y: 2, z: 4, core: 2. Of those that a mesh axis runs over, the one named last changes fastest.
Arguments:
- tokens: bfloat16 [4, 4096, 1536], P('wt', 'seq'), may hold values from -6 to 6
- norm_gain: float32 [1536], replicated, may hold values from 0.5 to 1.5
- in_weight: bfloat16 [1536, 6448], P('wt'), may hold values from -0.15625 to 0.15625
- conv_kernel: float32 [4, 3328], replicated, may hold values from -2 to 2
- conv_bias: float32 [3328], replicated, may hold values from -1.5 to 1.5
- step_bias: float32 [48], replicated, may hold values from -10 to -3
- decay_log: float32 [48], replicated, may hold values from 0 to 2.77
- skip_gain: float32 [48], replicated, may hold values from 0.5 to 1.5
- out_gain: float32 [3072], replicated, may hold values from 0.5 to 1.5
- out_weight: bfloat16 [3072, 1536], P('wt'), may hold values from -0.109375 to 0.109375
- cotangent: bfloat16 [4, 4096, 1536], P('wt', 'seq'), may hold values from -6 to 6
Outputs:
- mixed_out: bfloat16 [4, 4096, 1536], P('wt', 'seq')
- grad_tokens: float32 [4, 4096, 1536], P('wt', 'seq')
- grad_norm_gain: float32 [1536], replicated
- grad_in_weight: float32 [1536, 6448], P('wt')
- grad_conv_kernel: float32 [4, 3328], replicated
- grad_conv_bias: float32 [3328], replicated
- grad_step_bias: float32 [48], replicated
- grad_decay_log: float32 [48], replicated
- grad_skip_gain: float32 [48], replicated
- grad_out_gain: float32 [3072], replicated
- grad_out_weight: float32 [3072, 1536], P('wt')
All inputs are finite; a program needn't handle non-finite values.
Results may differ from a plain program's by a relative error of at most 0.013.
Values may be sent and summed in bfloat16 or wider, within the bound.
A program may use at most 320 MiB of HBM per device.

v0:
```python
import jax
import jax.numpy as jnp
from jax import lax
from jax.sharding import PartitionSpec as P

DI = 3072
HEADS = 48
HDIM = 64
NSTATE = 128
CONV = 4
GROUP = 256
CDIM = 3328


EPS = 1e-05
HIGH = lax.Precision.HIGHEST


def shifted(array, axis, by):
    peers = lax.axis_size(axis)
    pairs = [(i, i + by) for i in range(peers) if 0 <= i + by < peers]
    return lax.ppermute(array, axis, pairs)


def prefix(array, axis, combine, identity, reverse):
    peers, index = (lax.axis_size(axis), lax.axis_index(axis))
    everything = jax.tree.map(lambda part: lax.all_gather(part, axis), array)
    start = jax.tree.map(
        lambda part, zero: jnp.broadcast_to(jnp.asarray(zero, part.dtype), part.shape),
        array,
        identity,
    )

    def turn(k, before):
        at = peers - 1 - k if reverse else k
        reached = at > index if reverse else at < index
        new = combine(before, jax.tree.map(lambda part: part[at], everything))
        return jax.tree.map(lambda a, b: jnp.where(reached, a, b), new, before)

    return lax.fori_loop(0, peers, turn, start)


def normalize(inputs, norm_gain):
    return inputs * lax.rsqrt(jnp.mean(inputs * inputs, axis=-1, keepdims=True) + EPS) * norm_gain


def front(proj, prior, conv_kernel, conv_bias, step_bias, decay_log):
    length = proj.shape[0]
    gate_in = proj[:, :DI]
    conv_in = proj[:, DI : DI + CDIM]
    step_raw = proj[:, DI + CDIM :]
    padded = jnp.concatenate([prior, conv_in], axis=0)
    summed = conv_bias + sum((conv_kernel[k] * padded[k : k + length] for k in range(CONV)))
    conv_act = jax.nn.silu(summed)
    heads_in = conv_act[:, :DI].reshape(length, HEADS, HDIM)
    input_mat = conv_act[:, DI : DI + NSTATE]
    output_mat = conv_act[:, DI + NSTATE :]
    step_size = jax.nn.softplus(step_raw + step_bias)
    log_decay = -step_size * jnp.exp(decay_log)
    return (gate_in, heads_in, input_mat, output_mat, step_size, log_decay)


def block_step(state, piece):
    heads_in, input_mat, output_mat, step_size, log_decay = piece
    running = jnp.cumsum(log_decay, axis=0)
    spread = running[:, None, :] - running[None, :, :]
    row_ids = lax.broadcasted_iota(jnp.int32, spread.shape, 0)
    col_ids = lax.broadcasted_iota(jnp.int32, spread.shape, 1)
    decay = jnp.exp(jnp.where(row_ids >= col_ids, spread, -jnp.inf))
    scores = jnp.dot(output_mat, input_mat.T, precision=HIGH)
    mixing = scores[:, :, None] * decay * step_size[None, :, :]
    inside = jnp.einsum("tsh,shp->thp", mixing, heads_in, precision=HIGH)
    carried = jnp.exp(running)[:, :, None] * jnp.einsum(
        "tn,hpn->thp", output_mat, state, precision=HIGH
    )
    weight_end = jnp.exp(running[-1][None, :] - running) * step_size
    new_state = jnp.exp(running[-1])[:, None, None] * state + jnp.einsum(
        "shp,sn->hpn", weight_end[:, :, None] * heads_in, input_mat, precision=HIGH
    )
    return (new_state, inside + carried)


def inner(heads_in, input_mat, output_mat, step_size, log_decay):
    count = heads_in.shape[0] // GROUP
    pieces = tuple(
        (
            v.reshape((count, GROUP) + v.shape[1:])
            for v in (heads_in, input_mat, output_mat, step_size, log_decay)
        )
    )
    start = jnp.zeros((HEADS, HDIM, NSTATE), jnp.float32)
    final, outputs = lax.scan(jax.checkpoint(block_step), start, pieces)
    return (outputs.reshape(heads_in.shape), final, jnp.exp(jnp.sum(log_decay, axis=0)))


def cross(output_mat, log_decay, incoming):
    running = jnp.cumsum(log_decay, axis=0)
    return jnp.exp(running)[:, :, None] * jnp.einsum(
        "tn,hpn->thp", output_mat, incoming, precision=HIGH
    )


def finish(heads_in, scanned, gate_in, skip_gain, out_gain):
    length = heads_in.shape[0]
    scan_out = (scanned + skip_gain[:, None] * heads_in).reshape(length, DI)
    gated = scan_out * jax.nn.silu(gate_in)
    return gated * lax.rsqrt(jnp.mean(gated * gated, axis=-1, keepdims=True) + EPS) * out_gain


def carry_join(earlier, later):
    return (earlier[0] * later[0], later[0][:, None, None] * earlier[1] + later[1])


def carry_back(earlier, later):
    return (earlier[0] * later[0], later[1] + later[0][:, None, None] * earlier[1])


def shards(
    tokens,
    norm_gain,
    in_weight,
    conv_kernel,
    conv_bias,
    step_bias,
    decay_log,
    skip_gain,
    out_gain,
    out_weight,
    cotangent,
):
    inputs = tokens[0].astype(jnp.float32)
    in_all, out_all = (
        lax.all_gather(in_weight, "wt", axis=0, tiled=True),
        lax.all_gather(out_weight, "wt", axis=0, tiled=True),
    )
    normed, norm_pull = jax.vjp(normalize, inputs, norm_gain)
    normed_low = normed.astype(jnp.bfloat16)
    proj = jnp.dot(normed_low, in_all, preferred_element_type=jnp.float32).astype(jnp.bfloat16)
    rim_rows = proj[proj.shape[0] - (CONV - 1) :, DI : DI + CDIM]
    prior = shifted(rim_rows, "seq", 1)
    features, front_pull = jax.vjp(
        front,
        proj.astype(jnp.float32),
        prior.astype(jnp.float32),
        conv_kernel,
        conv_bias,
        step_bias,
        decay_log,
    )
    gate_in, heads_in, input_mat, output_mat, step_size, log_decay = features
    (local_out, local_state, device_decay), inner_pull = jax.vjp(
        inner, heads_in, input_mat, output_mat, step_size, log_decay
    )
    ones_start = jnp.ones((HEADS,), jnp.float32)
    zero_state = jnp.zeros((HEADS, HDIM, NSTATE), jnp.float32)
    passed = prefix((device_decay, local_state), "seq", carry_join, (ones_start, zero_state), False)
    incoming = passed[1]
    far_out, cross_pull = jax.vjp(cross, output_mat, log_decay, incoming)
    normed_out, finish_pull = jax.vjp(
        finish, heads_in, local_out + far_out, gate_in, skip_gain, out_gain
    )
    out_low = normed_out.astype(jnp.bfloat16)
    mixed = (inputs + jnp.dot(out_low, out_all, preferred_element_type=jnp.float32)).astype(
        jnp.bfloat16
    )
    upstream = cotangent[0]
    d_normed_out = jnp.dot(upstream, out_all.T, preferred_element_type=jnp.float32)
    dheads_a, d_scanned, d_gate, d_skip, d_outgain = finish_pull(d_normed_out)
    doutput_a, ddecay_a, d_incoming = cross_pull(d_scanned)
    returned = prefix((device_decay, d_incoming), "seq", carry_back, (ones_start, zero_state), True)
    d_leaving = returned[1]
    d_device = jnp.sum(incoming * d_leaving, axis=(1, 2))
    dheads_b, dinput_b, doutput_b, dstep_b, ddecay_b = inner_pull((d_scanned, d_leaving, d_device))
    d_proj, d_prior, d_kernel, d_cbias, d_sbias, d_dlog = front_pull(
        (d_gate, dheads_a + dheads_b, dinput_b, doutput_a + doutput_b, dstep_b, ddecay_a + ddecay_b)
    )
    rim_grad = shifted(d_prior.astype(jnp.bfloat16), "seq", -1).astype(d_prior.dtype)
    d_proj = d_proj.at[d_proj.shape[0] - (CONV - 1) :, DI : DI + CDIM].add(rim_grad)
    dproj_low = d_proj.astype(jnp.bfloat16)
    d_normed = jnp.dot(dproj_low, in_all.T, preferred_element_type=jnp.float32)
    dinput_norm, d_normgain = norm_pull(d_normed)
    grad_inputs = upstream.astype(jnp.float32) + dinput_norm
    grad_win = jnp.dot(normed_low.T, dproj_low, preferred_element_type=jnp.float32)
    grad_wout = jnp.dot(out_low.T, upstream, preferred_element_type=jnp.float32)
    part_in, part_out = (
        lax.psum_scatter(grad_win, "wt", scatter_dimension=0, tiled=True),
        lax.psum_scatter(grad_wout, "wt", scatter_dimension=0, tiled=True),
    )
    shard_in, shard_out = lax.psum((part_in, part_out), "seq")
    summed = lax.psum(
        (d_normgain, d_kernel, d_cbias, d_sbias, d_dlog, d_skip, d_outgain), ("seq", "wt")
    )
    return (
        mixed[None],
        grad_inputs[None],
        summed[0],
        shard_in,
        summed[1],
        summed[2],
        summed[3],
        summed[4],
        summed[5],
        summed[6],
        shard_out,
    )


def solution(mesh):
    return jax.shard_map(
        shards,
        mesh=mesh,
        in_specs=(
            P("wt", "seq", None),
            P(),
            P("wt", None),
            P(),
            P(),
            P(),
            P(),
            P(),
            P(),
            P("wt", None),
            P("wt", "seq", None),
        ),
        out_specs=(
            P("wt", "seq", None),
            P("wt", "seq", None),
            P(),
            P("wt", None),
            P(),
            P(),
            P(),
            P(),
            P(),
            P(),
            P("wt", None),
        ),
        check_vma=False,
    )
```

profile of v0, /device:TPU:0, one launch (start us, length us, event | category | flops | bytes accessed | tf_op | source)
XLA Modules:
  0.0 2267.2 jit_solution(6755199652584682475)
XLA Ops:
  11.7 125.6 %all-gather.8.cloned.1.call-done = bf16[1536,6448]{0,1:T(8,128)(2,1)} async-done(((bf16[384,6448]{0,1:T(8,128)(2,1)}), bf16[1536,6448]{0,1:T(8,128)(2,1)}) %all-gather.8.cloned.1.call-update) | async-done | bytes 19808272 | tf_op jit(solution)/shard_map/all_gather | solution.py:133
  137.2 19.6 fusion.152
  164.3 5.9 slice.170
  172.0 19.7 fusion.96
  198.1 8.2 reshape.374
  206.3 6.5 copy.266
  212.8 5.7 broadcast.183.clone2
  218.5 195.2 %while.72 = (s32[]{:T(128)}, f32[48,64,128]{2,1,0:T(8,128)S(1)}, f32[2,256,48,64]{1,0,3,2:T(2,128)}, f32[2,48,64,128]{3,2,1,0:T(8,128)}, f32[2,256,48]{1,2,0:T(8...) while((s32[]{:T(128)}, f32[48,64,128]{2,1,0:T(8,128)S(1)}, ...), condition=%wide.region_4.5_spmd.clone, body=%wide.region_1.4_spmd.clone.sunk | while | flops 4954165248 | bytes 38165476 | solution.py:92
  222.4 15.3 fusion.254
  241.4 4.9 copy.432
  246.3 63.6 %dynamic_update_slice.78 = f32[2,256,48,64]{1,0,3,2:T(2,128)} dynamic-update-slice(f32[2,256,48,64]{1,0,3,2:T(2,128)} %get-tuple-element.1264, f32[1,256,48,64]{1,0,3,2:T(1,128)} %copy.432, s32[]{:T(128)S(6)} %copy.444, s32[]{:T(128)} %constant.224.clone.1..sunk.1, s32[]{:T(128)} %constant.224.clone.1..sunk.1, s32[]{:T(128)} %constant.224.clone.1..sunk.1) | dynamic-update-slice | bytes 6291460 | tf_op jit(solution)/shard_map/jvp()/while/body/jit(dynamic_update_index_in_dim)/dynamic_update_slice | solution.py:92
  311.2 5.1 multiply_add_fusion.9
  319.7 15.3 fusion.254
  338.8 4.9 copy.432
  343.7 63.6 %dynamic_update_slice.78 = f32[2,256,48,64]{1,0,3,2:T(2,128)} dynamic-update-slice(f32[2,256,48,64]{1,0,3,2:T(2,128)} %get-tuple-element.1264, f32[1,256,48,64]{1,0,3,2:T(1,128)} %copy.432, s32[]{:T(128)S(6)} %copy.444, s32[]{:T(128)} %constant.224.clone.1..sunk.1, s32[]{:T(128)} %constant.224.clone.1..sunk.1, s32[]{:T(128)} %constant.224.clone.1..sunk.1) | dynamic-update-slice | bytes 6291460 | tf_op jit(solution)/shard_map/jvp()/while/body/jit(dynamic_update_index_in_dim)/dynamic_update_slice | solution.py:92
  408.5 5.1 multiply_add_fusion.9
  417.1 19.2 all-reduce.16
  437.9 9.1 reshape.377
  447.0 143.2 %all-gather.12.cloned.1.call-done = f32[384,64,128]{2,1,0:T(8,128)} async-done(((f32[48,64,128]{2,1,0:T(8,128)}), f32[384,64,128]{2,1,0:T(8,128)}) %all-gather.12.cloned.1.call-update) | async-done | bytes 12582928 | tf_op jit(solution)/shard_map/all_gather | solution.py:27
  590.2 15.2 while.73
  605.4 8.1 fusion.134
  613.5 12.3 multiply_add_fusion.3
  625.8 7.7 multiply_reduce_fusion.12
  633.5 20.8 all-gather.10.cloned.1.call-done
  654.2 12.8 multiply_reduce_fusion.8
  667.1 12.3 multiply_reduce_fusion.9
  682.1 6.3 fusion.102
  688.4 12.8 fusion.121
  702.1 8.5 reshape.383
  710.6 6.4 multiply_reduce_fusion.10
  717.1 5.0 reduce-window.80
  722.9 142.1 %all-gather.14.cloned.1.call-done = f32[384,64,128]{2,1,0:T(8,128)} async-done(((f32[48,64,128]{2,1,0:T(8,128)}), f32[384,64,128]{2,1,0:T(8,128)}) %all-gather.14.cloned.1.call-update) | async-done | bytes 12582928 | tf_op jit(solution)/shard_map/all_gather | solution.py:27
  865.0 16.5 while.74
  885.4 6.3 broadcast.183.clone
  891.8 365.8 %while.71 = (s32[]{:T(128)}, f32[48,64,128]{2,1,0:T(8,128)}, f32[2,256,48,64]{1,0,3,2:T(2,128)}, f32[2,256,128]{2,1,0:T(8,128)}, f32[2,256,128]{2,1,0:T(8,128)},...) while((s32[]{:T(128)}, f32[48,64,128]{2,1,0:T(8,128)}, ...), condition=%wide.region_27.28_spmd, body=%wide.region_14.27_spmd.sunk | while | flops 11245326336 | bytes 130753112 | solution.py:92
  898.1 6.5 constant_dynamic-slice_fusion.6
  915.3 4.6 multiply_reduce_fusion.18
  923.5 20.5 fusion.236
  948.7 7.3 multiply_reduce_fusion.20
  964.2 6.5 fusion.242
  976.8 7.4 fusion.240
  984.2 12.7 fusion.239
  1008.1 63.2 %dynamic_update_slice.75 = f32[2,256,48,64]{1,0,3,2:T(2,128)} dynamic-update-slice(f32[2,256,48,64]{1,0,3,2:T(2,128)} %get-tuple-element.1353, f32[1,256,48,64]{1,0,3,2:T(1,128)S(1)} %copy.424, s32[]{:T(128)S(6)} %sub.227, s32[]{:T(128)} %constant.224.clone.1..sunk, s32[]{:T(128)} %constant.224.clone.1..sunk, s32[]{:T(128)} %constant.224.clone.1..sunk) | dynamic-update-slice | bytes 6291460 | tf_op jit(solution)/shard_map/transpose(jvp())/while/body/jit(dynamic_update_index_in_dim)/dynamic_update_slice | solution.py:92
  1077.3 6.1 constant_dynamic-slice_fusion.6
  1094.0 4.6 multiply_reduce_fusion.18
  1102.2 20.5 fusion.236
  1127.4 7.2 multiply_reduce_fusion.20
  1142.8 6.5 fusion.242
  1155.6 7.4 fusion.240
  1163.1 12.4 fusion.239
  1186.6 63.2 %dynamic_update_slice.75 = f32[2,256,48,64]{1,0,3,2:T(2,128)} dynamic-update-slice(f32[2,256,48,64]{1,0,3,2:T(2,128)} %get-tuple-element.1353, f32[1,256,48,64]{1,0,3,2:T(1,128)S(1)} %copy.424, s32[]{:T(128)S(6)} %sub.227, s32[]{:T(128)} %constant.224.clone.1..sunk, s32[]{:T(128)} %constant.224.clone.1..sunk, s32[]{:T(128)} %constant.224.clone.1..sunk) | dynamic-update-slice | bytes 6291460 | tf_op jit(solution)/shard_map/transpose(jvp())/while/body/jit(dynamic_update_index_in_dim)/dynamic_update_slice | solution.py:92
  1272.4 25.2 %multiply_reduce_fusion.6 = (f32[3328]{0:T(1024)}, f32[3328]{0:T(1024)S(1)}, f32[3328]{0:T(1024)S(1)}, f32[3328]{0:T(1024)}, f32[3328]{0:T(1024)S(1)}, /*index=5*/f32[512,3328]{0,1:T(8,128)S(1)}) fusion(f32[512,3328]{0,1:T(8,128)} %slice.170, f32[3,3328]{0,1:T(8,128)} %copy-done.14, f32[512,6448]{0,1:T(8,128)} %get-tuple-element.990, ...), kind=kLoop, calls=%fused_computation.146 | loop fusion | flops 39173888 | bytes 34185216 | tf_op jit(solution)/shard_map/transpose(jvp())/reduce_sum | solution.py:53
  1297.6 9.9 broadcast_multiply_fusion
  1307.5 12.5 pad_add_fusion.1
  1320.9 4.7 split.9
  1333.0 10.3 pad_add_fusion
  1346.4 10.8 scatter-add.4
  1357.2 21.4 fusion.106
  1381.3 23.7 %fusion.111 = (f32[1536]{0:T(1024)}, f32[512]{0:T(512)S(1)}, f32[512,1536]{1,0:T(8,128)}) fusion(bf16[1,512,1536]{2,1,0:T(8,128)(2,1)S(1)} %copy-done.19, f32[512]{0:T(512)S(1)} %copy-done.54, f32[1536]{0:T(1024)S(1)} %copy-done.52, bf16[1536,6448]{0,1:T(8,128)(2,1)} %all-gather.8.cloned.1.call-done, f32[512,6448]{0,1:T(8,128)} %scatter-add.4), kind=kOutput, calls=%fused_computation.186 | convolution fusion | flops 10150631424 | bytes 37748736 | tf_op jit(solution)/shard_map/dot_general | solution.py:180
  1405.1 250.5 %reduce-scatter.3.cloned.1.call-done = f32[384,6448]{0,1:T(8,128)} async-done(((f32[1536,6448]{0,1:T(8,128)}), f32[384,6448]{0,1:T(8,128)}) %reduce-scatter.3.cloned.1.call-update) | async-done | bytes 9904144 | tf_op jit(solution)/shard_map/reduce_scatter | solution.py:186
  1656.3 11.1 fusion.120
  1670.0 116.8 %all-reduce.22.cloned.1.call-done = (f32[1536]{0:T(1024)}, f32[4,3328]{1,0:T(4,128)}, f32[3328]{0:T(1024)}, f32[48]{0:T(128)}, f32[48]{0:T(128)}, /*index=5*/f32[48]{0:T(128)}, f32[3072]{0:T(1024)}) async-done(((f32[1536]{0:T(1024)}, f32[4,3328]{1,0:T(4,128)}, f32[3328]{0:T(1024)}, f32[48]{0:T(128)}, f32[48]{0:T(128)}, /*index=5*/f32[48]{0:T(128)}, f32[3072]{0:T(1024)}), (f32[1536]{0:T(1024)}, ...) | async-done | bytes 85584 | tf_op jit(solution)/shard_map/psum | solution.py:190
  1786.8 457.9 %all-reduce.24.cloned.1.call-done = (f32[384,6448]{0,1:T(8,128)}, f32[768,1536]{1,0:T(8,128)}) async-done(((f32[384,6448]{0,1:T(8,128)}, f32[768,1536]{1,0:T(8,128)}), (f32[384,6448]{0,1:T(8,128)}, f32[768,1536]{1,0:T(8,128)})) %all-reduce.24.cloned.1.call-update) | async-done | bytes 14622736 | tf_op jit(solution)/shard_map/psum | solution.py:189
  2246.1 8.5 copy.504
  (402 shorter events, 219.7 us)
Async XLA Ops:
  7.2 130.0 %copy-start.18 = (bf16[1,512,1536]{2,1,0:T(8,128)(2,1)S(1)}, bf16[1,512,1536]{2,1,0:T(8,128)(2,1)}, u32[]{:S(2)}) copy-start(bf16[1,512,1536]{2,1,0:T(8,128)(2,1)} %param.21) | copy-start | bytes 4718596
  7.2 130.0 %copy-start.51 = (f32[1536]{0:T(1024)S(1)}, f32[1536]{0:T(1024)}, u32[]{:S(2)}) copy-start(f32[1536]{0:T(1024)} %param.22) | copy-start | bytes 18436
  7.2 130.0 %all-gather.8.cloned.1.call-start = ((), (), s32[]{:S(2)}) async-start(), calls=%async_computation.2 | async-start | bytes 24760320 | tf_op jit(solution)/shard_map/all_gather | solution.py:133
  7.9 582.3 %all-gather.12.cloned.1.call-start = ((), (), s32[]{:S(2)}) async-start(), calls=%async_computation.6 | async-start | bytes 14155776 | tf_op jit(solution)/shard_map/all_gather | solution.py:27
  8.7 154.0 %copy-start.59 = (f32[48]{0:T(128)}, f32[48]{0:T(128)S(1)}, u32[]{:S(2)}) copy-start(f32[48]{0:T(128)S(1)} %exp.117) | copy-start | bytes 580
  9.8 162.2 %copy-start.32 = (f32[3328]{0:T(1024)}, f32[3328]{0:T(1024)S(1)}, u32[]{:S(2)}) copy-start(f32[3328]{0:T(1024)S(1)} %get-tuple-element.876) | copy-start | bytes 39940
  9.8 162.2 %copy-start.34 = (f32[3328]{0:T(1024)}, f32[3328]{0:T(1024)S(1)}, u32[]{:S(2)}) copy-start(f32[3328]{0:T(1024)S(1)} %get-tuple-element.877) | copy-start | bytes 39940
  9.8 162.2 %copy-start.36 = (f32[3328]{0:T(1024)}, f32[3328]{0:T(1024)S(1)}, u32[]{:S(2)}) copy-start(f32[3328]{0:T(1024)S(1)} %get-tuple-element.878) | copy-start | bytes 39940
  9.8 162.2 %copy-start.38 = (f32[3328]{0:T(1024)}, f32[3328]{0:T(1024)S(1)}, u32[]{:S(2)}) copy-start(f32[3328]{0:T(1024)S(1)} %get-tuple-element.879) | copy-start | bytes 39940
  11.6 145.2 %copy-start.44 = (f32[512]{0:T(512)}, f32[512]{0:T(512)S(1)}, u32[]{:S(2)}) copy-start(f32[512]{0:T(512)S(1)} %fusion.114) | copy-start | bytes 6148
  11.6 145.2 %copy-start.53 = (f32[512]{0:T(512)}, f32[512]{0:T(512)S(1)}, u32[]{:S(2)}) copy-start(f32[512]{0:T(512)S(1)} %fusion.141) | copy-start | bytes 6148
  11.6 151.0 %copy-start.58 = (f32[48]{0:T(128)S(1)}, f32[48]{0:T(128)}, u32[]{:S(2)}) copy-start(f32[48]{0:T(128)} %param.26) | copy-start | bytes 580
  158.6 12.2 collective-permute-start
  172.0 19.8 copy-start.14
  218.5 197.2 %copy-start.66 = (u32[32]{0:T(128)S(1)}, u32[32]{0:T(128)}, u32[]{:S(2)}) copy-start(u32[32]{0:T(128)} %constant.272) | copy-start | bytes 388
  218.5 198.5 %copy-start.60 = (f32[48]{0:T(128)S(1)}, f32[48]{0:T(128)}, u32[]{:S(2)}) copy-start(f32[48]{0:T(128)} %get-tuple-element.964) | copy-start | bytes 580
  414.9 239.3 %all-gather.10.cloned.1.call-start = ((), (), s32[]{:S(2)}) async-start(), calls=%async_computation.3 | async-start | bytes 11796480 | tf_op jit(solution)/shard_map/all_gather | solution.py:134
  415.7 449.3 %all-gather.14.cloned.1.call-start = ((), (), s32[]{:S(2)}) async-start(), calls=%async_computation.7 | async-start | bytes 14155776 | tf_op jit(solution)/shard_map/all_gather | solution.py:27
  437.9 241.5 %copy-start.25 = (f32[512,48]{0,1:T(8,128)}, f32[512,48]{0,1:T(8,128)S(1)}, u32[]{:S(2)}) copy-start(f32[512,48]{0,1:T(8,128)S(1)} %bitcast_bitcast_fusion.3) | copy-start | bytes 294916
  625.8 28.5 %copy-start.48 = (f32[3072]{0:T(1024)S(1)}, f32[3072]{0:T(1024)}, u32[]{:S(2)}) copy-start(f32[3072]{0:T(1024)} %param.29) | copy-start | bytes 36868
  625.8 41.3 %slice-start.2 = ((s8[6815744]{0:T(1024)(128)(4,1)}), s8[2621440]{0:T(1024)(128)(4,1)S(1)}, s32[]{:S(2)}) async-start(s8[6815744]{0:T(1024)(128)(4,1)} %bitcast.437), calls=%async_computation.12 | async-start | bytes 5242880
  633.5 55.0 %copy-start.55 = (f32[512]{0:T(512)}, f32[512]{0:T(512)S(1)}, u32[]{:S(2)}) copy-start(f32[512]{0:T(512)S(1)} %fusion.142) | copy-start | bytes 6148
  654.2 12.8 slice-start.3
  654.2 12.8 copy-start.11
  688.4 716.7 %reduce-scatter.5.cloned.1.call-start = ((), (), s32[]{:S(2)}) async-start(), calls=%async_computation.5 | async-start | bytes 23592960 | tf_op jit(solution)/shard_map/reduce_scatter | solution.py:187
  701.3 954.3 %reduce-scatter.3.cloned.1.call-start = ((), (), s32[]{:S(2)}) async-start(), calls=%async_computation.4 | async-start | bytes 49520640 | tf_op jit(solution)/shard_map/reduce_scatter | solution.py:186
  722.1 142.8 %copy-start.29 = (f32[48,4,128]{2,0,1:T(8,128)}, f32[48,4,128]{2,0,1:T(8,128)S(1)}, u32[]{:S(2)}) copy-start(f32[48,4,128]{2,0,1:T(8,128)S(1)} %reduce-window.80) | copy-start | bytes 294916
  881.4 10.3 copy-start.8
  893.8 20.8 copy-start.12
  893.9 10.7 copy-start.3
  923.5 20.5 copy-start.17
  962.6 14.1 copy-start.15
  984.2 12.7 copy-start
  984.2 12.7 copy-start.16
  1002.6 68.7 %copy-start.23 = (f32[2,256,48]{1,0,2:T(2,128)S(1)}, f32[2,256,48]{1,0,2:T(2,128)}, u32[]{:S(2)}) copy-start(f32[2,256,48]{1,0,2:T(2,128)} %copy-done.22) | copy-start | bytes 294916 | tf_op jit(solution)/shard_map/transpose(jvp())/while
  1073.1 20.2 copy-start.12
  1073.1 10.3 copy-start.3
  1102.2 20.5 copy-start.17
  1141.2 14.3 copy-start.15
  1163.0 12.4 copy-start
  1163.0 12.4 copy-start.16
  1181.2 68.7 %copy-start.23 = (f32[2,256,48]{1,0,2:T(2,128)S(1)}, f32[2,256,48]{1,0,2:T(2,128)}, u32[]{:S(2)}) copy-start(f32[2,256,48]{1,0,2:T(2,128)} %copy-done.22) | copy-start | bytes 294916 | tf_op jit(solution)/shard_map/transpose(jvp())/while
  1272.4 25.2 %copy-start.33 = (f32[3328]{0:T(1024)S(1)}, f32[3328]{0:T(1024)}, u32[]{:S(2)}) copy-start(f32[3328]{0:T(1024)} %copy-done.32) | copy-start | bytes 39940
  1272.4 25.2 %copy-start.35 = (f32[3328]{0:T(1024)S(1)}, f32[3328]{0:T(1024)}, u32[]{:S(2)}) copy-start(f32[3328]{0:T(1024)} %copy-done.34) | copy-start | bytes 39940
  1272.4 25.2 %copy-start.37 = (f32[3328]{0:T(1024)S(1)}, f32[3328]{0:T(1024)}, u32[]{:S(2)}) copy-start(f32[3328]{0:T(1024)} %copy-done.36) | copy-start | bytes 39940
  1272.4 25.2 %copy-start.39 = (f32[3328]{0:T(1024)S(1)}, f32[3328]{0:T(1024)}, u32[]{:S(2)}) copy-start(f32[3328]{0:T(1024)} %copy-done.38) | copy-start | bytes 39940
  1320.9 9.1 copy-start.7
  1320.9 9.2 copy-start.9
  1320.9 10.3 copy-start.30
  1328.8 14.5 collective-permute-start.1
  1343.3 13.9 copy-start.52
  1343.3 13.9 copy-start.54
  1378.6 408.2 %all-reduce.22.cloned.1.call-start = ((), (), s32[]{:S(2)}) async-start(), calls=%async_computation.8 | async-start | bytes 183296 | tf_op jit(solution)/shard_map/psum | solution.py:190
  1405.0 839.7 %all-reduce.24.cloned.1.call-start = ((), (), s32[]{:S(2)}) async-start(), calls=%async_computation.9 | async-start | bytes 29245440 | tf_op jit(solution)/shard_map/psum | solution.py:189
  1656.3 11.1 copy-start.45
  1656.3 11.1 copy-start.24
  1656.3 11.1 copy-start.27
  2246.0 8.5 copy-start.41
  2246.0 9.2 copy-start.47
  2246.0 9.8 copy-start.65
  2246.0 10.3 copy-start.64
  2246.0 10.8 copy-start.63
  2246.0 11.3 copy-start.50
  2246.1 11.9 copy-start.21
  (28 other events, 93.8 us)
Sparse Core Ops, SparseCore 0:
  9.6 127.5 all-gather.7
  415.0 175.1 all-gather.11
  591.8 62.4 all-gather.9
  688.5 176.4 all-gather.13
  867.4 137.6 reduce-scatter.4
  1378.7 276.8 reduce-scatter.2
  1663.2 123.5 all-reduce.21
  1791.1 453.5 all-reduce.23
where the time goes:
time: 2300 us; the launch traced here: 2270 us
  waiting for transfers between devices  1260 us (55%)
  local copies, waits for them, and re-layouts  453 us (20%)
  matrix products  303 us (13%)
  other arithmetic  202 us (9%)
    psum x1, waiting for transfers between devices, shards(): shard_in, shard_out = lax.psum((part_in, part_out), 'seq')  458 us
    all_gather x2, waiting for transfers between devices, prefix(): everything = jax.tree.map(lambda part: lax.all_gather(part, axis), array)  285 us
    dynamic_update_slice x12, local copies, waits for them, and re-layouts, inner(): final, outputs = lax.scan(jax.checkpoint(block_step), start, pieces)  274 us
    reduce_scatter x1, waiting for transfers between devices, shards(): lax.psum_scatter(grad_win, 'wt', scatter_dimension=0, tiled=True)  251 us
    all_gather x1, waiting for transfers between devices, shards(): lax.all_gather(in_weight, 'wt', axis=0, tiled=True)  126 us
    psum x1, waiting for transfers between devices, shards(): lax.psum((d_normgain, d_kernel, d_cbias, d_sbias, d_dlog, d_skip, d_outga...  117 us
    dot_general x6, matrix products, block_step(): inside = jnp.einsum('tsh,shp->thp', mixing, heads_in, precision=HIGH)  96.7 us
  transfers between devices with their start and end apart: 10, of which 7 were waited for; matrix products, arithmetic and copies ran while one was open for 28% of the time, Pallas kernels for 0%

commit v1 on v0

v1 whole, which is shorter than its diff:
```python
import jax
import jax.numpy as jnp
import numpy as np
from jax import lax
from jax.experimental import pallas as pl
from jax.experimental.pallas import tpu as pltpu
from jax.sharding import PartitionSpec as P

DI = 3072
HEADS = 48
HDIM = 64
NSTATE = 128
CONV = 4
CDIM = 3328
EDGE = 16
BLOCK = 128
GROUP = 8
WIDE = GROUP * HDIM
STEPS = HEADS // GROUP
LONG = (STEPS + 1) * WIDE
LANES = 128
TILE = 512
FINE = 256
SHORT = 64
AHEAD = 4
LAG = 2
LAST = 320
PARTS = 4
DM = 1536
PART = DM // PARTS
OUT_PART = DI // PARTS
SLOTS = 16
FEW = 4
SLACK = 2
MESH = pl.DeviceIdType.MESH

EPS = 1e-05
F32 = jnp.float32
LOW = jnp.bfloat16


def dot(a, b, ca, cb):
    return lax.dot_general(a, b, (((ca,), (cb,)), ((), ())), preferred_element_type=F32)


def nn(a, b):
    return dot(a, b, 1, 0)


def nt(a, b):
    return dot(a, b, 1, 1)


def tn(a, b):
    return dot(a, b, 0, 0)


def exact(a, b):
    return jnp.dot(a, b, precision=lax.Precision.HIGHEST, preferred_element_type=F32)


def halves(v):
    high = v.astype(LOW)
    return jnp.concatenate([high, (v - high.astype(F32)).astype(LOW)], axis=1)


def softplus(v):
    z = jnp.exp(-jnp.abs(v))
    small = z * (1.0 - z * (0.5 - z * (1.0 / 3.0 - z * 0.25)))
    return jnp.maximum(v, 0.0) + jnp.where(z < 0.01, small, jnp.log(1.0 + z))


def rows_cols(shape):
    return (lax.broadcasted_iota(jnp.int32, shape, 0), lax.broadcasted_iota(jnp.int32, shape, 1))


class Begin:
    def __init__(self, proj_ref, taps_ref, heads_ref, e2_ref, x_ref, bc_ref, dt_ref, rb_ref, rt_ref, er_ref, ew_ref, d2_ref, ed_ref, state_ref, pad_ref, wd_ref):
        self.proj, self.taps, self.heads, self.e2 = proj_ref, taps_ref, heads_ref, e2_ref
        self.x, self.bc, self.dt, self.rb, self.rt = x_ref, bc_ref, dt_ref, rb_ref, rt_ref
        self.er, self.ew, self.d2, self.ed, self.state = er_ref, ew_ref, d2_ref, ed_ref, state_ref
        self.pad, self.wd = pad_ref, wd_ref
        self.length = x_ref.shape[0]

    def convolved(self, first, width):
        self.pad[:, :width] = self.proj[:, first : first + width].astype(F32)
        total = self.taps[CONV : CONV + 1, first : first + WIDE]
        for k in range(CONV):
            at = EDGE - CONV + 1 + k
            total = total + self.taps[k : k + 1, first : first + WIDE] * self.pad[at : at + self.length, :]
        return total * jax.nn.sigmoid(total)

    def sizes(self):
        length = self.length
        self.pad[...] = jnp.zeros_like(self.pad)
        act = self.convolved(DI, CDIM + HEADS - DI)
        self.bc[...] = act[:, : 2 * NSTATE].astype(LOW)
        raw = self.pad[EDGE:, 2 * NSTATE : 2 * NSTATE + LANES]
        used = lax.broadcasted_iota(jnp.int32, raw.shape, 1) < HEADS
        dt = jnp.where(used, softplus(jnp.where(used, raw + self.heads[0:1, :], 0.0)), 0.0)
        self.dt[...] = dt
        self.d2[...] = halves(dt)
        decay = -dt * jnp.exp(self.heads[1:2, :])
        ids, jds = rows_cols((BLOCK, BLOCK))
        lower = (ids >= jds).astype(F32)
        before = jnp.zeros((1, LANES), F32)
        whole = []
        for c in range(length // BLOCK):
            at = slice(c * BLOCK, (c + 1) * BLOCK)
            run = exact(lower, decay[at])
            last = run[BLOCK - 1 : BLOCK]
            for j in range(STEPS):
                turned = jnp.concatenate([run[:, GROUP * j :], run[:, : GROUP * j]], axis=1) if j else run
                self.rb[at, j * LANES : (j + 1) * LANES] = turned
            self.rt[:, at] = run.T
            self.er[at, :] = halves(jnp.exp(run))
            self.ew[at, :] = halves(jnp.exp(last - run))
            whole.append(run + before)
            self.ed[at, :] = halves(jnp.exp(run + before))
            before = before + last
        for c in range(length // BLOCK):
            at = slice(c * BLOCK, (c + 1) * BLOCK)
            self.wd[at, :] = halves(jnp.exp(before - whole[c]) * dt[at])

    def block(self, j):
        at = slice(j * WIDE, (j + 1) * WIDE)
        x = self.convolved(j * WIDE, WIDE).astype(LOW)
        self.x[:, at] = x
        e2 = self.e2[:, at]
        weighed = (x.astype(F32) * nn(self.wd[...], e2)).astype(LOW)
        self.state[0:NSTATE, at] = tn(self.bc[:, :NSTATE], weighed).astype(LOW)
        decay = nn(self.ed[self.length - 16 : self.length, :], e2)[15:16, :]
        high = decay.astype(LOW).astype(F32)
        ids = lax.broadcasted_iota(jnp.int32, (16, WIDE), 0)
        self.state[NSTATE : NSTATE + 16, at] = jnp.where(ids == 0, high, jnp.where(ids == 1, decay - high, 0.0)).astype(LOW)


class Stages:
    def __init__(self, ref, sem):
        self.ref, self.sem, self.count = ref, sem, ref.shape[0]
        self.flying = [None] * self.count
        self.turn = 0

    def put(self, value, target):
        at = self.turn % self.count
        if self.flying[at] is not None:
            self.flying[at].wait()
        self.ref[at] = value
        self.flying[at] = pltpu.make_async_copy(self.ref.at[at], target, self.sem.at[at])
        self.flying[at].start()
        self.turn += 1

    def rest(self):
        for one in self.flying:
            if one is not None:
                one.wait()


class Inside:
    def __init__(self, x_ref, bc_ref, rb_ref, rt_ref, er_ref, ew_ref, d2_ref, e2_ref, held_ref, y_out, states_out, ys, states):
        self.x, self.bc, self.rb, self.rt = x_ref, bc_ref, rb_ref, rt_ref
        self.er, self.ew, self.d2, self.e2, self.held = er_ref, ew_ref, d2_ref, e2_ref, held_ref
        self.y_out, self.states_out, self.ys, self.states = y_out, states_out, ys, states
        self.blocks = x_ref.shape[0] // BLOCK

    def turn(self, at):
        if at < STEPS * self.blocks:
            self.block(at // self.blocks, at % self.blocks)

    def block(self, j, c):
        at, own = slice(c * BLOCK, (c + 1) * BLOCK), slice(j * WIDE, (j + 1) * WIDE)
        ids, jds = rows_cols((BLOCK, BLOCK))
        left = lax.broadcasted_iota(jnp.int32, (BLOCK, LANES), 1) < HDIM
        input_mat, output_mat = self.bc[at, :NSTATE], self.bc[at, NSTATE:]
        e2 = self.e2[:, own]
        grow, leave = nn(self.er[at, :], e2), nn(self.ew[at, :], e2)
        x = self.x[at, own].astype(F32) * nn(self.d2[at, :], e2)
        scores = jnp.where(ids >= jds, nt(output_mat, input_mat), 0.0)
        held = self.held[...] if c else jnp.zeros_like(self.held)
        self.states.put(held.astype(LOW), self.states_out.at[c, :, own])
        carried = grow * nn(output_mat, held.astype(LOW))
        parts = []
        for pair in range(GROUP // 2):
            lanes = slice(pair * LANES, (pair + 1) * LANES)
            piece = x[:, lanes]
            mixed = []
            for head in (2 * pair, 2 * pair + 1):
                column = self.rb[at, j * LANES + head : j * LANES + head + 1]
                spread = column - self.rt[j * GROUP + head : j * GROUP + head + 1, at]
                mixed.append((scores * jnp.exp(jnp.minimum(spread, 0.0))).astype(LOW))
            both = jnp.concatenate([jnp.where(left, piece, 0.0), jnp.where(left, 0.0, piece)], axis=0)
            parts.append(nn(jnp.concatenate(mixed, axis=1), both.astype(LOW)) + carried[:, lanes])
        self.ys.put(jnp.concatenate(parts, axis=1), self.y_out.at[at, own])
        self.held[...] = held * grow[BLOCK - 1 : BLOCK, :] + tn(input_mat, (x * leave).astype(LOW))


def middle_kernel(y_ref, bc_ref, in_ref, ed_ref, e2_ref, x_ref, gate_ref, dno_ref, gains_ref, low_ref, dy_ref, dgate_ref, sums_ref, din_ref, out_ref, gated_ref):
    @pl.when(pl.program_id(0) == 0)
    def _():
        sums_ref[...] = jnp.zeros_like(sums_ref)
        din_ref[...] = jnp.zeros_like(din_ref)

    output_mat = bc_ref[:, NSTATE:]
    part = DI // PARTS
    tiles = []
    for j in range(PARTS):
        there = relative(j)
        tiles.append((slice(j * part, (j + 1) * part), pl.ds(pl.multiple_of(there * part, LANES), part)))
    square = jnp.zeros((BLOCK, 1), F32)
    cross = jnp.zeros((BLOCK, 1), F32)
    for at, there in tiles:
        far = nn(ed_ref[...], e2_ref[:, at]) * nn(output_mat, in_ref[:, at])
        out = y_ref[:, at] + far + gains_ref[1:2, at] * x_ref[:, at].astype(F32)
        gate = gate_ref[:, at].astype(F32)
        gated = out * gate * jax.nn.sigmoid(gate)
        out_ref[:, at] = out
        gated_ref[:, at] = gated
        square = square + jnp.sum(gated * gated, axis=1, keepdims=True)
        cross = cross + jnp.sum(gated * (dno_ref[:, there] * gains_ref[0:1, at]), axis=1, keepdims=True)
    scale = lax.rsqrt(square * (1.0 / DI) + EPS)
    pull = scale * scale * scale * (cross * (1.0 / DI))
    for at, there in tiles:
        gate = gate_ref[:, at].astype(F32)
        gated, out, gain = gated_ref[:, at], out_ref[:, at], gains_ref[0:1, at]
        shape = jax.nn.sigmoid(gate)
        unit = gated * scale
        low_ref[:, there] = (unit * gain).astype(LOW)
        dno = dno_ref[:, there]
        dgated = scale * (dno * gain) - gated * pull
        dy = dgated * (gate * shape)
        dy_ref[:, at] = dy.astype(LOW)
        dgate_ref[:, at] = (dgated * out * (shape * (1.0 + gate * (1.0 - shape)))).astype(LOW)
        sums_ref[0:1, at] += jnp.sum(dno * unit, axis=0, keepdims=True)
        sums_ref[1:2, at] += jnp.sum(dy * x_ref[:, at].astype(F32), axis=0, keepdims=True)
        din_ref[:, at] += tn(output_mat, (dy * nn(ed_ref[...], e2_ref[:, at])).astype(LOW))


def middle(y, bc, incoming, ed, e2, x, gate, dno, gains, length):
    rows = lambda c: (c, 0)
    fixed = lambda c: (0, 0)
    return pl.pallas_call(
        middle_kernel,
        grid=(length // BLOCK,),
        in_specs=[
            pl.BlockSpec((BLOCK, DI), rows),
            pl.BlockSpec((BLOCK, 2 * NSTATE), rows),
            pl.BlockSpec((NSTATE, DI), fixed),
            pl.BlockSpec((BLOCK, 2 * LANES), rows),
            pl.BlockSpec((2 * LANES, DI), fixed),
            pl.BlockSpec((BLOCK, DI), rows),
            pl.BlockSpec((BLOCK, DI), rows),
            pl.BlockSpec((BLOCK, DI), rows),
            pl.BlockSpec((8, DI), fixed),
        ],
        out_specs=[
            pl.BlockSpec((BLOCK, DI), rows),
            pl.BlockSpec((BLOCK, DI), rows),
            pl.BlockSpec((BLOCK, DI), rows),
            pl.BlockSpec((8, DI), fixed),
            pl.BlockSpec((NSTATE, DI), fixed),
        ],
        out_shape=[
            jax.ShapeDtypeStruct((length, DI), LOW),
            jax.ShapeDtypeStruct((length, DI), LOW),
            jax.ShapeDtypeStruct((length, DI), LOW),
            jax.ShapeDtypeStruct((8, DI), F32),
            jax.ShapeDtypeStruct((NSTATE, DI), F32),
        ],
        scratch_shapes=[pltpu.VMEM((BLOCK, DI), F32), pltpu.VMEM((BLOCK, DI), F32)],
        compiler_params=pltpu.CompilerParams(vmem_limit_bytes=48 << 20),
        cost_estimate=pl.CostEstimate(flops=12 << 30, bytes_accessed=32 << 20, transcendentals=4 << 20),
        name="middle",
    )(y, bc, incoming, ed, e2, x, gate, dno, gains)


def spot():
    wt, seq = lax.axis_index("wt"), lax.axis_index("seq")
    return wt // 2, wt % 2, seq % 2


def relative(block):
    x, core, _ = spot()
    high, low = block // 2, block % 2
    return 2 * (core + low - 2 * core * low) + (x + high - 2 * x * high)


def across_bit(axis, bit):
    index = lax.axis_index(axis)
    return {axis: index + bit - 2 * bit * ((index // bit) % 2)}


def greet(devices):
    barrier = pltpu.get_barrier_semaphore()
    for device in devices:
        pl.semaphore_signal(barrier, inc=1, device_id=device, device_id_type=MESH)
    pl.semaphore_wait(barrier, len(devices))


class Piece:
    def __init__(self, source, near, mine, pair, twin, half, sems, at):
        bit = 1 + at % 2
        part = pl.multiple_of((lax.axis_index("seq") // bit) % 2 * half, 16)
        own, xs, xr, ys, yr, ts, tr, keep = sems
        rows = lambda ref: ref.at[pl.ds(part, half), :]
        self.own = pltpu.make_async_copy(source, mine, own.at[at])
        self.x = self.remote(rows(source), rows(near), xs.at[at], xr.at[at], across_bit("wt", 2))
        self.y = self.remote(rows(near), rows(near), ys.at[at], yr.at[at], across_bit("seq", bit))
        self.twin = self.remote(pair, twin, ts.at[at], tr.at[at], across_bit("wt", 1))

    def remote(self, source, target, send, recv, device):
        return pltpu.make_async_remote_copy(src_ref=source, dst_ref=target, send_sem=send, recv_sem=recv, device_id=device, device_id_type=MESH)


def gather_sems(count):
    return [pltpu.SemaphoreType.DMA((count,)) for _ in range(8)]


def enter_kernel(tok_ref, gain_ref, kernel_ref, bias_ref, step_ref, log_ref, e2_ref, w_ref, taps_ref, heads_ref, proj_ref, normed_ref, x_ref, bc_ref, dt_ref, rb_ref, rt_ref, er_ref, ew_ref, d2_ref, ed_ref, state_ref, all_ref, wide_ref, last_ref, edge_ref, pad_ref, wd_ref, edge_sem, *sems):
    length = tok_ref.shape[0]
    begin = Begin(proj_ref, taps_ref, heads_ref, e2_ref, x_ref, bc_ref, dt_ref, rb_ref, rt_ref, er_ref, ew_ref, d2_ref, ed_ref, state_ref, pad_ref, wd_ref)
    seq, peers = lax.axis_index("seq"), lax.axis_size("seq")
    following, previous = {"seq": lax.rem(seq + 1, peers)}, {"seq": lax.rem(seq + peers - 1, peers)}
    greet([across_bit("wt", 1), across_bit("wt", 2), across_bit("seq", 1), across_bit("seq", 2), following, previous])
    edge = pltpu.make_async_remote_copy(src_ref=tok_ref.at[length - EDGE : length, :], dst_ref=edge_ref, send_sem=edge_sem.at[0], recv_sem=edge_sem.at[1], device_id=following, device_id_type=MESH)
    edge.start()
    count = CDIM // TILE
    pieces, products, keeps = [], [], []

    def add(target, first, rows):
        pieces.append(Piece(w_ref.at[pl.ds(first, rows), :], target.at[:, PART : 2 * PART], target.at[:, :PART], target.at[:, : 2 * PART], target.at[:, 2 * PART :], rows // 2, sems, len(pieces)))
        products.append(None)

    def multiply(target, columns, skip, then):
        keep = pltpu.make_async_copy(target.at[skip:, :], all_ref.at[columns, :], sems[-1].at[len(keeps)])
        keeps.append(keep)

        def product():
            keep.start()
            proj_ref[:, columns] = nt(normed_ref[...], target[skip:, :]).astype(LOW)
            then()

        products[-1] = product

    add(last_ref, DI + CDIM + HEADS - LAST, LAST)
    multiply(last_ref, slice(count * TILE, CDIM + HEADS), LAST - (CDIM + HEADS - count * TILE), begin.sizes)
    for c in range(count):
        for first in range(c * TILE, (c + 1) * TILE, FINE):
            add(wide_ref.at[first : first + FINE, :], DI + first, FINE)
        multiply(wide_ref.at[c * TILE : (c + 1) * TILE, :], slice(c * TILE, (c + 1) * TILE), 0, lambda c=c: begin.block(c))
    for piece in pieces:
        piece.own.start()
    for piece in pieces[:AHEAD]:
        piece.x.start()

    def norm(v):
        v = v.astype(F32)
        return (v * lax.rsqrt(jnp.mean(v * v, axis=-1, keepdims=True) + EPS) * gain_ref[0:1, :]).astype(LOW)

    def place(at, v):
        for b in range(PARTS):
            normed_ref[at, pl.ds(pl.multiple_of(relative(b) * PART, LANES), PART)] = v[:, b * PART : (b + 1) * PART]

    taps_ref[...] = jnp.zeros_like(taps_ref)
    taps_ref[0:CONV, :CDIM] = kernel_ref[...]
    taps_ref[CONV : CONV + 1, :CDIM] = bias_ref[...]
    heads_ref[...] = jnp.zeros_like(heads_ref)
    heads_ref[0:1, :HEADS] = step_ref[...]
    heads_ref[1:2, :HEADS] = log_ref[...]
    place(slice(EDGE, EDGE + length), norm(tok_ref[...]))
    edge.wait()
    place(slice(0, EDGE), norm(jnp.where(seq == 0, 0.0, edge_ref[...].astype(F32))))
    travel_on(pieces, products)
    for keep in keeps:
        keep.wait()


def travel_on(pieces, products, ahead=AHEAD, between=None):
    count = len(pieces)
    for t in range(count + 2 * LAG):
        if t < count:
            pieces[t].x.wait_recv()
            pieces[t].y.start()
            if t + ahead < count:
                pieces[t + ahead].x.start()
        if 0 <= t - LAG < count:
            pieces[t - LAG].y.wait_recv()
            pieces[t - LAG].own.wait()
            pieces[t - LAG].twin.start()
        if 0 <= t - 2 * LAG < count:
            pieces[t - 2 * LAG].twin.wait_recv()
            if products[t - 2 * LAG] is not None:
                products[t - 2 * LAG]()
        if between is not None:
            between(t)
    for piece in pieces:
        piece.x.wait_send()
        piece.y.wait_send()
        piece.twin.wait_send()


def enter(tokens, gain, conv_kernel, conv_bias, step_bias, decay_log, e2, weight):
    length, columns = tokens.shape[0], CDIM + HEADS
    vmem, hbm = pl.BlockSpec(memory_space=pltpu.VMEM), pl.BlockSpec(memory_space=pl.ANY)
    shapes = [
        ((8, LONG), F32),
        ((8, LANES), F32),
        ((length + EDGE, columns), LOW),
        ((length + EDGE, DM), LOW),
        ((length, DI), LOW),
        ((length, 2 * NSTATE), LOW),
        ((length, LANES), F32),
        ((length, LANES * STEPS), F32),
        ((LANES, length), F32),
        ((length, 2 * LANES), LOW),
        ((length, 2 * LANES), LOW),
        ((length, 2 * LANES), LOW),
        ((length, 2 * LANES), LOW),
        ((NSTATE + 16, DI), LOW),
        ((columns, DM), LOW),
    ]
    return pl.pallas_call(
        enter_kernel,
        in_specs=[vmem] * 7 + [hbm],
        out_specs=[vmem] * (len(shapes) - 1) + [hbm],
        out_shape=[jax.ShapeDtypeStruct(shape, kind) for shape, kind in shapes],
        scratch_shapes=[
            pltpu.VMEM((CDIM // TILE * TILE, DM), LOW),
            pltpu.VMEM((LAST, DM), LOW),
            pltpu.VMEM((EDGE, DM), LOW),
            pltpu.VMEM((length + EDGE, WIDE), F32),
            pltpu.VMEM((length, 2 * LANES), LOW),
            pltpu.SemaphoreType.DMA((2,)),
        ]
        + gather_sems(CDIM // TILE * (TILE // FINE) + 1),
        compiler_params=pltpu.CompilerParams(vmem_limit_bytes=56 << 20, collective_id=0, has_side_effects=True),
        cost_estimate=pl.CostEstimate(flops=40 << 30, bytes_accessed=30 << 20, transcendentals=0),
        name="enter",
    )(tokens, gain, conv_kernel, conv_bias, step_bias, decay_log, e2, weight)


class Passing:
    def __init__(self, later, total, factor, reach, held, send, recv, met, send_sem, recv_sem):
        self.later, self.total, self.factor, self.reach, self.held = later, total, factor, reach, held
        self.send, self.recv, self.met, self.send_sem, self.recv_sem = send, recv, met, send_sem, recv_sem
        self.bits = seq_bits()

    def columns(self, j):
        return pl.ds(pl.multiple_of(j * WIDE, WIDE), WIDE)

    def copy(self, k, j):
        at = self.columns(j)
        return pltpu.make_async_remote_copy(src_ref=self.send.at[:, at], dst_ref=self.recv.at[k, :, at], send_sem=self.send_sem.at[k, j], recv_sem=self.recv_sem.at[k, j], device_id=across_bit("seq", self.bits[k]), device_id_type=MESH)

    def start(self, k, j):
        at = self.columns(j)
        self.send[0:NSTATE, at] = self.total[:, at].astype(LOW)
        if not self.later:
            factor = self.factor[0:1, at]
            high = factor.astype(LOW).astype(F32)
            ids = lax.broadcasted_iota(jnp.int32, (16, WIDE), 0)
            self.send[NSTATE : NSTATE + 16, at] = jnp.where(ids == 0, high, jnp.where(ids == 1, factor - high, 0.0)).astype(LOW)
        self.copy(k, j).start()

    def finish(self, k, j):
        self.copy(k, j).wait()
        at = self.columns(j)
        bit = self.bits[k]
        second = (lax.axis_index("seq") // bit) % 2
        takes = second == (0 if self.later else 1)
        other = self.recv[k, 0:NSTATE, at].astype(F32)
        if self.later:
            met = self.met[k : k + 1, at]
        else:
            rows = self.recv[k, NSTATE : NSTATE + 16, at].astype(F32)
            met = rows[0:1] + rows[1:2]
            self.met[k : k + 1, at] = met
        total, factor, reach = self.total[:, at], self.factor[0:1, at], self.reach[0:1, at]
        self.held[:, at] = self.held[:, at] + jnp.where(takes, reach, 0.0) * other
        self.reach[0:1, at] = jnp.where(takes, reach * met, reach)
        if k + 1 < len(self.bits):
            self.total[:, at] = jnp.where(takes, factor, 1.0) * other + jnp.where(takes, 1.0, met) * total
            self.factor[0:1, at] = factor * met
            self.start(k + 1, j)

    def due(self, k, j):
        last = len(self.bits) - 1
        return 2 + 3 * k + 2 * j if k < last else 2 + 3 * last + 3 * j

    def step(self, t):
        for k in range(len(self.bits)):
            for j in range(STEPS):
                if t == self.due(k, j):
                    self.finish(k, j)

    def rest(self, t):
        for late in range(t, self.due(len(self.bits) - 1, STEPS - 1) + 1):
            self.step(late)


def gates_kernel(normed_ref, up_ref, state_ref, x_ref, bc_ref, rb_ref, rt_ref, er_ref, ew_ref, d2_ref, e2_ref, w_ref, o_ref, incoming_ref, met_ref, y_out, states_out, gate_out, dno_out, wall_ref, wide_ref, deep_ref, total_ref, factor_ref, reach_ref, held_ref, send_ref, recv_ref, own_ref, y_ref, states_ref, gate_ref, dno_ref, ss_sem, sr_sem, deep_sem, stage_sem, *sems):
    stages = [Stages(ref, stage_sem.at[i]) for i, ref in enumerate((y_ref, states_ref, gate_ref, dno_ref))]
    local = Inside(x_ref, bc_ref, rb_ref, rt_ref, er_ref, ew_ref, d2_ref, e2_ref, own_ref, y_out, states_out, stages[0], stages[1])
    greet([across_bit("wt", 1), across_bit("wt", 2)] + [across_bit("seq", bit) for bit in seq_bits()])
    passing = Passing(False, total_ref, factor_ref, reach_ref, held_ref, send_ref, recv_ref, met_ref, ss_sem, sr_sem)
    total_ref[...] = state_ref[0:NSTATE, :].astype(F32)
    rows = state_ref[NSTATE : NSTATE + 16, :].astype(F32)
    factor_ref[0:1, :] = rows[0:1] + rows[1:2]
    reach_ref[...] = jnp.ones_like(reach_ref)
    held_ref[...] = jnp.zeros_like(held_ref)
    met_ref[...] = jnp.zeros_like(met_ref)
    met_ref[7:8, :] = factor_ref[0:1, :]
    for j in range(STEPS):
        passing.start(0, j)
    pieces, products, keeps = [], [], []

    for c in range(DI // FINE):
        rows = slice(c * FINE, (c + 1) * FINE)
        target = wide_ref.at[rows, :]
        pieces.append(Piece(w_ref.at[rows, :], target.at[:, PART : 2 * PART], target.at[:, :PART], target.at[:, : 2 * PART], target.at[:, 2 * PART :], FINE // 2, sems, len(pieces)))
        keeps.append(pltpu.make_async_copy(target, wall_ref.at[rows, :], sems[-1].at[c]))

        def product(rows=rows, keep=keeps[-1]):
            keep.start()
            stages[2].put(nt(normed_ref[EDGE:, :], wide_ref[rows, :]).astype(LOW), gate_out.at[:, rows])

        products.append(product)

    for c in range(OUT_PART // SHORT):
        rows = slice(c * SHORT, (c + 1) * SHORT)
        pieces.append(Piece(o_ref.at[rows, :], deep_ref.at[1, rows, :], deep_ref.at[0, rows, :], deep_ref.at[0:2, rows, :], deep_ref.at[2:4, rows, :], SHORT // 2, sems, len(pieces)))
        products.append(None)
        if (c + 1) * SHORT % FINE == 0:
            first = (c + 1) * SHORT - FINE
            mine = [pltpu.make_async_copy(deep_ref.at[b, first : first + FINE, :], wall_ref.at[pl.ds(DI + b * OUT_PART + first, FINE), :], deep_sem.at[first // FINE, b]) for b in range(PARTS)]
            keeps.extend(mine)

            def product(first=first, mine=mine):
                for b in range(PARTS):
                    mine[b].start()
                    at = b * OUT_PART + first
                    stages[3].put(nt(up_ref[...], deep_ref[b, first : first + FINE, :]), dno_out.at[:, at : at + FINE])

            products[-1] = product

    for piece in pieces:
        piece.own.start()
    for piece in pieces[:AHEAD]:
        piece.x.start()

    def between(t):
        passing.step(t)
        local.turn(t)

    travel_on(pieces, products, between=between)
    for t in range(len(pieces) + 2 * LAG, STEPS * local.blocks):
        local.turn(t)
    passing.rest(len(pieces) + 2 * LAG)
    for stage in stages:
        stage.rest()
    incoming_ref[...] = held_ref[...].astype(LOW)
    for keep in keeps:
        keep.wait()


def gates(normed, upstream, state, x, bc, rb, rt, er, ew, d2, e2, weight, out_weight):
    length = upstream.shape[0]
    bits = len(seq_bits())
    vmem, hbm = pl.BlockSpec(memory_space=pltpu.VMEM), pl.BlockSpec(memory_space=pl.ANY)
    dma = pltpu.SemaphoreType.DMA
    return pl.pallas_call(
        gates_kernel,
        in_specs=[vmem] * 11 + [hbm, hbm],
        out_specs=[vmem, vmem] + [hbm] * 5,
        out_shape=[
            jax.ShapeDtypeStruct((NSTATE, DI), LOW),
            jax.ShapeDtypeStruct((8, DI), F32),
            jax.ShapeDtypeStruct((length, DI), F32),
            jax.ShapeDtypeStruct((length // BLOCK, NSTATE, DI), LOW),
            jax.ShapeDtypeStruct((length, DI), LOW),
            jax.ShapeDtypeStruct((length, DI), F32),
            jax.ShapeDtypeStruct((2 * DI, DM), LOW),
        ],
        scratch_shapes=[
            pltpu.VMEM((DI, DM), LOW),
            pltpu.VMEM((PARTS, OUT_PART, DM), LOW),
            pltpu.VMEM((NSTATE, DI), F32),
            pltpu.VMEM((8, DI), F32),
            pltpu.VMEM((8, DI), F32),
            pltpu.VMEM((NSTATE, DI), F32),
            pltpu.VMEM((NSTATE + 16, DI), LOW),
            pltpu.VMEM((bits, NSTATE + 16, DI), LOW),
            pltpu.VMEM((NSTATE, WIDE), F32),
            pltpu.VMEM((2, BLOCK, WIDE), F32),
            pltpu.VMEM((2, NSTATE, WIDE), LOW),
            pltpu.VMEM((2, length, FINE), LOW),
            pltpu.VMEM((2, length, FINE), F32),
            dma((bits, STEPS)),
            dma((bits, STEPS)),
            dma((OUT_PART // FINE, PARTS)),
            dma((4, 2)),
        ]
        + gather_sems(DI // FINE + OUT_PART // SHORT),
        compiler_params=pltpu.CompilerParams(vmem_limit_bytes=58 << 20, collective_id=1, has_side_effects=True),
        cost_estimate=pl.CostEstimate(flops=50 << 30, bytes_accessed=50 << 20, transcendentals=0),
        name="gates",
    )(normed, upstream, state, x, bc, rb, rt, er, ew, d2, e2, weight, out_weight)


def seq_bits():
    bits, bit = [], 1
    while bit < lax.axis_size("seq"):
        bits.append(bit)
        bit *= 2
    return bits


ROWS = 128
LEAST = 16


class Reducer:
    def __init__(self, out, gate, conv, din, dout, held, core, sx, rx, near, res, load_sem, keep_sem, send_sem, recv_sem, parts):
        self.out, self.gate, self.conv, self.din, self.dout = out, gate, conv, din, dout
        self.held, self.core, self.sx, self.rx, self.near, self.res = held, core, sx, rx, near, res
        self.load_sem, self.keep_sem, self.send_sem, self.recv_sem, self.parts = load_sem, keep_sem, send_sem, recv_sem, parts
        bits = seq_bits()
        seq = lax.axis_index("seq")
        self.steps = len(bits)
        self.halved = halved_bits()
        self.partners = [across_bit("wt", 1), across_bit("wt", 2)] + [across_bit("seq", bit) for bit in bits]
        self.second = [(seq // bit) % 2 for bit in bits]
        self.bases, self.sizes = [0], [ROWS]
        for bit in bits[: self.halved]:
            size = self.sizes[-1] // 2
            self.bases.append(self.bases[-1] + ((seq // bit) % 2) * size)
            self.sizes.append(size)
        self.stages = 2 + self.steps + self.halved
        self.out_count = PARTS * (OUT_PART // ROWS)
        self.gate_count = DI // ROWS
        self.columns = CDIM + HEADS
        self.count = self.out_count + self.gate_count + -(-self.columns // ROWS)
        self.total = self.count + SLACK * self.stages + 1

    def rows_at(self, j):
        return pl.ds(pl.multiple_of(self.bases[j], LEAST), self.sizes[j])

    def kinds(self, c, act):
        first_gate, first_conv = self.out_count, self.out_count + self.gate_count

        @pl.when(c < first_gate)
        def _():
            first = pl.multiple_of((c // PARTS) * ROWS, 16)
            columns = pl.ds(pl.multiple_of((c % PARTS) * PART, LANES), PART)
            act([self.out.at[pl.ds(b * OUT_PART + first, ROWS), columns] for b in range(PARTS)], lambda: self.dout.at[pl.ds(first, ROWS), columns])

        @pl.when(jnp.logical_and(c >= first_gate, c < first_conv))
        def _():
            first = pl.multiple_of((c - first_gate) * ROWS, 16)
            act([self.gate.at[pl.ds(first, ROWS), :]], lambda: self.din.at[pl.ds(first, ROWS), :])

        @pl.when(c >= first_conv)
        def _():
            first = pl.multiple_of(jnp.minimum((c - first_conv) * ROWS, self.columns - ROWS), 16)
            act([self.conv.at[pl.ds(first, ROWS), :]], lambda: self.din.at[pl.ds(DI + first, ROWS), :])

    def load(self, c):
        few = lax.rem(c, FEW)

        def act(sources, target):
            width = DM // len(sources)
            for b, source in enumerate(sources):
                pltpu.make_async_copy(source, self.held.at[few, :, b * width : (b + 1) * width], self.load_sem.at[few]).start()

        self.kinds(c, act)

    def exchange(self, s, slot, few):
        if s == 0:
            source, target = self.held.at[few, :, 2 * PART :], self.core.at[few]
        elif s == 1:
            source, target = self.sx.at[few], self.rx.at[few]
        elif s < 2 + self.steps:
            source, target = self.parts[3 * (s - 2)].at[few], self.parts[3 * (s - 2) + 1].at[few]
        else:
            j = self.stages - 1 - s
            source = target = self.res.at[slot, self.rows_at(j + 1), :]
        partner = self.partners[s] if s < 2 + self.steps else self.partners[2 + self.stages - 1 - s]
        return pltpu.make_async_remote_copy(src_ref=source, dst_ref=target, send_sem=self.send_sem.at[s, few], recv_sem=self.recv_sem.at[s, few], device_id=partner, device_id_type=MESH)

    def loaded(self, few):
        pltpu.make_async_copy(self.gate.at[0:ROWS, :], self.held.at[few], self.load_sem.at[few]).wait()

    def kept(self, slot):
        return pltpu.make_async_copy(self.res.at[slot], self.din.at[0:ROWS, :], self.keep_sem.at[slot])

    def combine(self, s, slot, few):
        if s == 0:
            self.near[few] = self.held[few, :, :PART].astype(F32) + self.core[few, :, :PART].astype(F32)
            self.sx[few] = (self.held[few, :, PART : 2 * PART].astype(F32) + self.core[few, :, PART:].astype(F32)).astype(LOW)
        elif s == 1:
            self.lay(self.near[few] + self.rx[few].astype(F32), 0, slot, few)
        elif s < 2 + self.steps:
            j = s - 2
            mine = self.parts[3 * j + 2][few] if j < self.halved else self.parts[3 * j][few].astype(F32)
            self.lay(mine + self.parts[3 * j + 1][few].astype(F32), j + 1, slot, few)

    def lay(self, value, j, slot, few):
        if j == self.steps:
            self.res[slot, self.rows_at(self.halved), :] = value.astype(LOW)
        elif j < self.halved:
            size = self.sizes[j + 1]
            low, high = value[:size], value[size:]
            second = self.second[j] == 1
            self.parts[3 * j][few] = jnp.where(second, low, high).astype(LOW)
            self.parts[3 * j + 2][few] = jnp.where(second, high, low)
        else:
            self.parts[3 * j][few] = value.astype(LOW)

    def write(self, c, slot):
        self.kinds(c, lambda sources, target: pltpu.make_async_copy(self.res.at[slot], target(), self.keep_sem.at[slot]).start())

    def step(self, t):
        steady = jnp.logical_and(t > SLACK * self.stages, t < self.count)

        @pl.when(steady)
        def _():
            slots = [(lax.rem(t - SLACK * s, SLOTS), lax.rem(t - SLACK * s, FEW)) for s in range(self.stages + 1)]
            self.kept(lax.rem(t - SLACK * self.stages - 1, SLOTS)).wait()
            for s in range(self.stages, 0, -1):
                self.exchange(s - 1, *slots[s]).wait()
            self.loaded(slots[0][1])
            for s in range(self.stages, 0, -1):
                self.combine(s - 1, *slots[s])
            for s in range(1, self.stages):
                self.exchange(s, *slots[s]).start()
            self.exchange(0, *slots[0]).start()
            self.write(t - SLACK * self.stages, slots[self.stages][0])

        @pl.when(jnp.logical_not(steady))
        def _():
            c = t - SLACK * self.stages - 1

            @pl.when(jnp.logical_and(c >= 0, c < self.count))
            def _():
                self.kept(lax.rem(c, SLOTS)).wait()

            for s in range(self.stages, -1, -1):
                c = t - SLACK * s

                @pl.when(jnp.logical_and(c >= 0, c < self.count))
                def _(c=c, s=s):
                    slot, few = lax.rem(c, SLOTS), lax.rem(c, FEW)
                    if s > 0:
                        self.exchange(s - 1, slot, few).wait()
                        self.combine(s - 1, slot, few)
                    else:
                        self.loaded(few)
                    if s < self.stages:
                        self.exchange(s, slot, few).start()
                    else:
                        self.write(c, slot)

        @pl.when(t + 1 < self.count)
        def _():
            self.load(t + 1)


def halved_bits():
    count, rows = 0, ROWS
    while count < len(seq_bits()) and rows > LEAST:
        count, rows = count + 1, rows // 2
    return count


BLOCKS = 4
PER = 2
HALF = BLOCKS // PER
TURNS = HALF + 1
NEAR_STEPS, BACK_STEPS, EDGE_STEPS, DOT_STEPS, GATE_STEPS = STEPS * HALF, STEPS * TURNS + 1, 1, STEPS + 1, STEPS
BACK_AT = NEAR_STEPS
EDGE_AT = BACK_AT + BACK_STEPS
DOT_AT = EDGE_AT + EDGE_STEPS
PULL_AT = DOT_AT + DOT_STEPS
PULL_STEPS = 2 * GATE_STEPS + DOT_STEPS
LAST_AT = PULL_AT + PULL_STEPS
ALL_STEPS = LAST_AT + 1
PACE = ((0, NEAR_STEPS, 17), (BACK_AT, BACK_STEPS, 23), (EDGE_AT, EDGE_STEPS, 2), (DOT_AT, DOT_STEPS, 5), (PULL_AT, PULL_STEPS, 30))
DONE = sum(turns for _, _, turns in PACE)


def clip(v, low, high):
    return jnp.minimum(jnp.maximum(v, low), high)


def paced(g):
    done = 0
    for first, steps, turns in PACE:
        done = done + (turns * clip(g - first, 0, steps)) // steps
    return done


def head_block(g):
    near = jnp.minimum(g // HALF, STEPS)
    over = near // STEPS
    return near * (1 - over) + over * clip((g - BACK_AT) // TURNS, 0, STEPS - 1)


def rear_kernel(pc_ref, x_ref, dy_ref, bc_ref, rb_ref, rt_ref, er_ref, ew_ref, d2_ref, ed_ref, dt_ref, e2_ref, et_ref, states_ref, in_ref, taps_ref, skip_ref, heads_ref, met_ref, normed_ref, tok_ref, up_ref, gain_ref, sums_ref, low_ref, dgate_ref, wgate_ref, wconv_ref, din_ref, gout_ref, ggate_ref, sum_in_ref, sum_out_ref, small_ref, dtok_ref, mixed_ref, gconv_ref, pad_ref, dact_ref, dheld_ref, direct_ref, dconv_ref, dscores_ref, dbc_ref, ddt_ref, q_ref, v_ref, ends_ref, crossed_ref, stage_ref, rim_ref, rim_got_ref, one_sem, total_ref, factor_ref, reach_ref, held_ref, psend_ref, precv_ref, ps_sem, pr_sem, vsend_ref, vrecv_ref, vs_sem, vr_sem, r_held, r_core, r_sx, r_rx, r_near, r_res, load_sem, keep_sem, send_sem, recv_sem, *parts):
    g = pl.program_id(0)
    length = x_ref.shape[0]
    seq, peers = lax.axis_index("seq"), lax.axis_size("seq")
    following, previous = {"seq": lax.rem(seq + 1, peers)}, {"seq": lax.rem(seq + peers - 1, peers)}
    reducer = Reducer(gout_ref, ggate_ref, gconv_ref, sum_in_ref, sum_out_ref, r_held, r_core, r_sx, r_rx, r_near, r_res, load_sem, keep_sem, send_sem, recv_sem, parts)
    passing = Passing(True, total_ref, factor_ref, reach_ref, held_ref, psend_ref, precv_ref, met_ref, ps_sem, pr_sem)
    rounds = len(passing.bits)
    block = head_block(g)
    edge = pltpu.make_async_remote_copy(src_ref=rim_ref, dst_ref=rim_got_ref, send_sem=one_sem.at[0], recv_sem=one_sem.at[1], device_id=previous, device_id_type=MESH)

    @pl.when(g == 0)
    def _():
        greet(reducer.partners + [following, previous])
        first = pltpu.make_async_copy(din_ref, total_ref, one_sem.at[2])
        first.start()
        for ref in (dscores_ref, dbc_ref, ddt_ref, q_ref, v_ref, ends_ref, crossed_ref, held_ref):
            ref[...] = jnp.zeros_like(ref)
        reach_ref[...] = jnp.ones_like(reach_ref)
        factor_ref[0:1, :] = met_ref[7:8, :]
        first.wait()
        for j in range(STEPS):
            passing.start(0, j)
        reducer.load(jnp.int32(0))

    for k in range(rounds - 1):
        since = g - (1 + 2 * k)

        @pl.when(jnp.logical_and(since >= 0, since < STEPS))
        def _(k=k, since=since):
            passing.finish(k, since)

    def near_block(c):
        at = pl.ds(pl.multiple_of(c * BLOCK, BLOCK), BLOCK)
        ids, jds = rows_cols((BLOCK, BLOCK))
        suffix = (ids >= jds).astype(LOW)
        left = lax.broadcasted_iota(jnp.int32, (BLOCK, LANES), 1) < HDIM
        scores = jnp.where(ids <= jds, nt(bc_ref[at, :NSTATE], bc_ref[at, NSTATE:]), 0.0)
        dy = dy_ref[at, :]
        sized = x_ref[at, :].astype(F32) * nn(d2_ref[at, :], e2_ref[...])
        total = jnp.zeros((BLOCK, BLOCK), F32)
        rows = []
        for pair in range(GROUP // 2):
            lanes = slice(pair * LANES, (pair + 1) * LANES)
            piece, dpiece = sized[:, lanes], dy[:, lanes]
            both = jnp.concatenate([jnp.where(left, piece, 0.0), jnp.where(left, 0.0, piece)], axis=0).astype(LOW)
            meets = nn(both, dpiece.T)
            mixed, kept = [], []
            for half in range(2):
                head = 2 * pair + half
                spread = rt_ref[head : head + 1, at] - rb_ref[at, head : head + 1]
                decay = jnp.exp(jnp.minimum(spread, 0.0))
                meet = meets[half * BLOCK : (half + 1) * BLOCK] * decay
                total = total + meet
                mixed.append((scores * decay).astype(LOW))
                kept.append((meet * scores).astype(LOW))
            later = nn(jnp.concatenate(kept, axis=0), suffix)
            for half in range(2):
                one = later[half * BLOCK : (half + 1) * BLOCK]
                rows.append(jnp.sum(jnp.where(ids < jds, one, 0.0), axis=0, keepdims=True))
            none = jnp.zeros_like(dpiece)
            both = jnp.concatenate([jnp.where(left, dpiece, none), jnp.where(left, none, dpiece)], axis=0)
            direct_ref[block, at, lanes] = nn(jnp.concatenate(mixed, axis=1), both)
        dscores_ref[c] += total
        crossed_ref[pl.ds(pl.multiple_of(block * GROUP, GROUP), GROUP), at] = jnp.concatenate(rows, axis=0)

    @pl.when(g < NEAR_STEPS)
    def _():
        @pl.loop(0, PER)
        def _(i):
            near_block((g % HALF) * PER + i)

    turn = g - BACK_AT
    part = turn % TURNS
    going = jnp.logical_and(turn >= 0, turn < STEPS * TURNS)

    @pl.when(jnp.logical_and(going, part == 0))
    def _():
        passing.finish(rounds - 1, block)
        dheld_ref[...] = held_ref[:, passing.columns(block)]

    def back_block(c):
        at = pl.ds(pl.multiple_of(c * BLOCK, BLOCK), BLOCK)
        input_mat, output_mat = bc_ref[at, :NSTATE], bc_ref[at, NSTATE:]
        e2, et = e2_ref[...], et_ref[...]
        grow, leave, size = nn(er_ref[at, :], e2), nn(ew_ref[at, :], e2), nn(d2_ref[at, :], e2)
        prior = pl.ds(pl.multiple_of(jnp.maximum(c * BLOCK - 16, 0), 16), 16)
        reach = nn(ed_ref[prior, :], e2)[15:16, :]
        reach = jnp.where(c == 0, 1.0, reach)
        state = states_ref[c].astype(F32) + reach * in_ref[...].astype(F32)
        state_low = state.astype(LOW)
        x = x_ref[at, :].astype(F32)
        dy = dy_ref[at, :].astype(F32)
        dheld = dheld_ref[...]
        dheld_low = dheld.astype(LOW)
        grown = (dy * grow).astype(LOW)
        pulled = nn(input_mat, dheld_low) * leave
        dbc_ref[at, :NSTATE] += nt((x * size * leave).astype(LOW), dheld_low)
        dbc_ref[at, NSTATE:] += nt(grown, state_low)
        carried = nn(output_mat, state_low) * grow
        q_ref[at, :] += nn((dy * carried).astype(LOW), et)
        v_ref[at, :] += nn((x * pulled).astype(LOW), et)
        last = grow[BLOCK - 1 : BLOCK, :]
        ends = jnp.sum(state * dheld, axis=0, keepdims=True) * last
        ends_ref[c] += nn(jnp.broadcast_to(ends, (16, WIDE)).astype(LOW), et)[:8]
        dheld_ref[...] = dheld * last + tn(output_mat, grown)
        direct = direct_ref[block, at, :] + pulled
        ddt_ref[at, :] += nn((x * direct).astype(LOW), et)
        dact_ref[at, :] = size * direct + skip_ref[0:1, :] * dy

    @pl.when(jnp.logical_and(going, part < HALF))
    def _():
        @pl.loop(0, PER)
        def _(i):
            back_block(BLOCKS - 1 - (part * PER + i))

    @pl.when(turn == STEPS * TURNS)
    def _():
        ids, jds = rows_cols((BLOCK, BLOCK))
        upper = (ids <= jds).astype(F32)
        under = (ids > jds).astype(F32)
        rate = jnp.exp(heads_ref[1:2, :])
        dstep_bias = jnp.zeros((1, LANES), F32)
        ddecay_log = jnp.zeros((1, LANES), F32)
        for c in range(BLOCKS):
            at = slice(c * BLOCK, (c + 1) * BLOCK)
            dscores = jnp.where(ids <= jds, dscores_ref[c], 0.0).astype(LOW)
            dact_ref[at, :NSTATE] = dbc_ref[at, :NSTATE] + nn(dscores, bc_ref[at, NSTATE:])
            dact_ref[at, NSTATE : 2 * NSTATE] = dbc_ref[at, NSTATE:] + tn(dscores, bc_ref[at, :NSTATE])
            dt = dt_ref[at, :]
            ddecay = crossed_ref[:, at].T + exact(upper, q_ref[at, :]) + exact(under, v_ref[at, :] * dt) + ends_ref[c][0:1, :]
            draw = ddt_ref[at, :] - ddecay * rate
            ddecay_log = ddecay_log - jnp.sum(ddecay * dt, axis=0, keepdims=True) * rate
            raw = pc_ref[EDGE + c * BLOCK : EDGE + (c + 1) * BLOCK, 2 * NSTATE : 2 * NSTATE + LANES].astype(F32)
            used = lax.broadcasted_iota(jnp.int32, raw.shape, 1) < HEADS
            draw = draw * jax.nn.sigmoid(jnp.where(used, raw + heads_ref[0:1, :], 0.0))
            dstep_bias = dstep_bias + jnp.sum(draw, axis=0, keepdims=True)
            dact_ref[at, 2 * NSTATE : 2 * NSTATE + LANES] = draw
            dact_ref[at, 2 * NSTATE + LANES :] = jnp.zeros((BLOCK, LANES), F32)
        ends_ref[0] = jnp.broadcast_to(dstep_bias, (8, LANES))
        ends_ref[1] = jnp.broadcast_to(ddecay_log, (8, LANES))

    @pl.when(jnp.logical_or(jnp.logical_and(going, part == HALF), turn == STEPS * TURNS))
    def _():
        here = turn // TURNS
        at = pl.ds(pl.multiple_of(here * WIDE, WIDE), WIDE)
        taps = taps_ref[:, at]
        pad_ref[...] = pc_ref[...].astype(F32)
        summed = taps[CONV : CONV + 1]
        for k in range(CONV):
            first = EDGE - CONV + 1 + k
            summed = summed + taps[k : k + 1] * pad_ref[first : first + length, :]
        shape = jax.nn.sigmoid(summed)
        dsum = dact_ref[0:length, :] * (shape * (1.0 + summed * (1.0 - shape)))
        dtap = [jnp.sum(dsum * pad_ref[EDGE - CONV + 1 + k : EDGE - CONV + 1 + k + length, :], axis=0, keepdims=True) for k in range(CONV)]
        dtap.append(jnp.sum(dsum, axis=0, keepdims=True))
        vsend_ref[0, :, at] = jnp.concatenate(dtap + [jnp.zeros((8 - len(dtap), WIDE), F32)], axis=0)
        rim_ref[:, at] = dsum[:16].astype(LOW)
        keep = dact_ref[0:length, :]
        dact_ref[0:length, :] = dsum
        dact_ref[length:, :] = jnp.zeros_like(dact_ref[length:, :])
        result = taps[CONV - 1 : CONV] * dsum
        for k in range(CONV - 1):
            by = CONV - 1 - k
            result = result + taps[k : k + 1] * dact_ref[by : by + length, :]
        lane = lax.broadcasted_iota(jnp.int32, (1, WIDE), 1)
        raw_part = jnp.logical_and(turn == STEPS * TURNS, lane >= 2 * NSTATE)
        dconv_ref[:, at] = jnp.where(raw_part, keep, result).astype(LOW)

    @pl.when(turn == STEPS * TURNS)
    def _():
        edge.start()

    @pl.when(g == EDGE_AT)
    def _():
        edge.wait()
        bottom = slice(length - 16, length)
        inner = seq < peers - 1
        for j in range(STEPS + 1):
            at = slice(j * WIDE, min((j + 1) * WIDE, CDIM))
            got = rim_got_ref[:, at].astype(F32)
            ids = lax.broadcasted_iota(jnp.int32, got.shape, 0)
            extra = jnp.zeros_like(got)
            for i in range(CONV - 1):
                row = sum(taps_ref[k : k + 1, at] * got[i - k : i - k + 1] for k in range(i + 1))
                extra = jnp.where(ids == 16 - CONV + 1 + i, row, extra)
            extra = jnp.where(inner, extra, 0.0)
            dconv_ref[bottom, at] = (dconv_ref[bottom, at].astype(F32) + extra).astype(LOW)

    dot_turn = g - DOT_AT

    def stored(k):
        return pltpu.make_async_copy(stage_ref, gconv_ref.at[pl.ds(pl.multiple_of(k * WIDE, WIDE), WIDE), :], one_sem.at[2])

    @pl.when(jnp.logical_and(dot_turn >= 1, dot_turn <= DOT_STEPS))
    def _():
        stored(dot_turn - 1).wait()

    @pl.when(jnp.logical_and(dot_turn >= 0, dot_turn < DOT_STEPS))
    def _():
        columns = pl.ds(pl.multiple_of(dot_turn * WIDE, WIDE), WIDE)
        stage_ref[...] = tn(dconv_ref[:, columns], normed_ref[EDGE:, :]).astype(LOW)
        stored(dot_turn).start()

    pull = g - PULL_AT

    thirds = [slice(i * WIDE, (i + 1) * WIDE) for i in range(DM // WIDE)]
    mixed_out = pltpu.make_async_copy(stage_ref, mixed_ref, one_sem.at[2])

    @pl.when(pull == 0)
    def _():
        for i, at in enumerate(thirds):
            direct_ref[i] = tok_ref[:, at].astype(F32)

    @pl.when(jnp.logical_and(pull >= 0, pull < GATE_STEPS))
    def _():
        for i, at in enumerate(thirds):
            direct_ref[i] += nn(low_ref[...], wgate_ref[:, at])

    @pl.when(pull == GATE_STEPS)
    def _():
        for i, at in enumerate(thirds):
            stage_ref[:, at] = direct_ref[i].astype(LOW)
        mixed_out.start()
        direct_ref[0:PARTS] = jnp.zeros_like(direct_ref[0:PARTS])

    def add_pull(left, weight):
        for b in range(PARTS):
            direct_ref[b, :, :PART] += nn(left, weight[:, b * PART : (b + 1) * PART])

    @pl.when(jnp.logical_and(pull >= GATE_STEPS, pull < 2 * GATE_STEPS))
    def _():
        add_pull(dgate_ref[...], wgate_ref[...])

    @pl.when(jnp.logical_and(pull >= 2 * GATE_STEPS, pull < PULL_STEPS))
    def _():
        k = pull - 2 * GATE_STEPS
        columns = pl.ds(pl.multiple_of(k * WIDE, WIDE), WIDE)
        ids = lax.broadcasted_iota(jnp.int32, (WIDE, DM), 0)
        weight = wconv_ref[...]
        weight = jnp.where(ids < CDIM + HEADS - k * WIDE, weight, jnp.zeros_like(weight))
        add_pull(dconv_ref[:, columns], weight)

    def normed_out(b):
        return pltpu.make_async_copy(direct_ref.at[relative(b), :, 0:PART], dtok_ref.at[:, b * PART : (b + 1) * PART], one_sem.at[3 + b])

    meets = len(reducer.partners)

    def swap(k):
        return pltpu.make_async_remote_copy(src_ref=vsend_ref.at[k], dst_ref=vrecv_ref.at[k], send_sem=vs_sem.at[k], recv_sem=vr_sem.at[k], device_id=reducer.partners[k], device_id_type=MESH)

    @pl.when(g == LAST_AT)
    def _():
        blocks = [slice(b * PART, (b + 1) * PART) for b in range(PARTS)]
        square = jnp.zeros((length, 1), F32)
        cross = jnp.zeros((length, 1), F32)
        for b, at in enumerate(blocks):
            u = tok_ref[:, at].astype(F32)
            square = square + jnp.sum(u * u, axis=1, keepdims=True)
            cross = cross + jnp.sum(direct_ref[relative(b), :, :PART] * gain_ref[0:1, at] * u, axis=1, keepdims=True)
        rate = lax.rsqrt(square * (1.0 / DM) + EPS)
        pulled = rate * rate * rate * (cross * (1.0 / DM))
        for b, at in enumerate(blocks):
            u = tok_ref[:, at].astype(F32)
            there = relative(b)
            d_normed = direct_ref[there, :, :PART]
            vsend_ref[0, 5:6, at] = jnp.sum(d_normed * (u * rate), axis=0, keepdims=True)
            direct_ref[there, :, :PART] = up_ref[:, at].astype(F32) + rate * (d_normed * gain_ref[0:1, at]) - u * pulled
            normed_out(b).start()
        vsend_ref[0, 6:7, :DI] = sums_ref[0:1, :]
        vsend_ref[0, 7:8, :DI] = sums_ref[1:2, :]
        vsend_ref[0, 6:7, DI : DI + LANES] = ends_ref[0][0:1]
        vsend_ref[0, 7:8, DI : DI + LANES] = ends_ref[1][0:1]

        swap(0).start()

    @pl.loop(paced(g), paced(g + 1) + (g // LAST_AT) * (reducer.total - DONE))
    def _(t):
        reducer.step(t)
        for k in range(meets):

            @pl.when(t == DONE + 2 * (k + 1))
            def _(k=k):
                swap(k).wait()
                value = vsend_ref[k] + vrecv_ref[k]
                if k + 1 < meets:
                    vsend_ref[k + 1] = value
                    swap(k + 1).start()
                else:
                    small_ref[...] = value

    @pl.when(g == LAST_AT)
    def _():
        for b in range(PARTS):
            normed_out(b).wait()
        mixed_out.wait()


def rear(proj, x, dy, bc, rb, rt, er, ew, d2, ed, dt, e2, et, states, incoming, taps, skip, heads, met, normed, tokens, upstream, gain, sums, low, dgate, wide_all, conv_all, din, grad_out, grad_gate):
    length = x.shape[0]
    bits, halved = len(seq_bits()), halved_bits()
    hbm = pl.BlockSpec(memory_space=pl.ANY)
    back_block = lambda g: clip((g - BACK_AT) // TURNS, 0, STEPS)
    part_block = lambda g: clip((g - BACK_AT) // TURNS, 0, STEPS - 1)

    def whole(array):
        return pl.BlockSpec(array.shape, lambda g: (0,) * array.ndim, pipeline_mode=pl.Buffered(1))

    shares = []
    for j in range(bits):
        shape = (FEW, max(ROWS >> (j + 1), LEAST), PART)
        shares += [pltpu.VMEM(shape, LOW), pltpu.VMEM(shape, LOW), pltpu.VMEM(shape, F32)]
    dma = pltpu.SemaphoreType.DMA
    stages, meets = 2 + bits + halved, 2 + bits
    return pl.pallas_call(
        rear_kernel,
        grid=(ALL_STEPS,),
        in_specs=[
            pl.BlockSpec((length + EDGE, WIDE), lambda g: (0, back_block(g))),
            pl.BlockSpec((length, WIDE), lambda g: (0, head_block(g))),
            pl.BlockSpec((length, WIDE), lambda g: (0, head_block(g))),
            whole(bc),
            pl.BlockSpec((length, LANES), lambda g: (0, jnp.minimum(g // HALF, STEPS - 1))),
            pl.BlockSpec((GROUP, length), lambda g: (jnp.minimum(g // HALF, STEPS - 1), 0)),
            whole(er),
            whole(ew),
            whole(d2),
            whole(ed),
            whole(dt),
            pl.BlockSpec((2 * LANES, WIDE), lambda g: (0, head_block(g))),
            pl.BlockSpec((WIDE, LANES), lambda g: (part_block(g), 0)),
            pl.BlockSpec((length // BLOCK, NSTATE, WIDE), lambda g: (0, 0, part_block(g))),
            pl.BlockSpec((NSTATE, WIDE), lambda g: (0, part_block(g))),
            whole(taps),
            pl.BlockSpec((8, WIDE), lambda g: (0, part_block(g))),
            whole(heads),
            whole(met),
            whole(normed),
            whole(tokens),
            whole(upstream),
            whole(gain),
            whole(sums),
            pl.BlockSpec((length, WIDE), lambda g: (0, clip(g - PULL_AT, 0, GATE_STEPS - 1))),
            pl.BlockSpec((length, WIDE), lambda g: (0, clip(g - PULL_AT - GATE_STEPS, 0, GATE_STEPS - 1))),
            pl.BlockSpec((WIDE, DM), lambda g: ((clip(g - PULL_AT, 0, 2 * GATE_STEPS - 1) + GATE_STEPS) % (2 * GATE_STEPS), 0)),
            pl.BlockSpec((WIDE, DM), lambda g: (clip(g - PULL_AT - 2 * GATE_STEPS, 0, DOT_STEPS - 1), 0)),
            hbm,
            hbm,
            hbm,
        ],
        out_specs=[hbm, hbm, pl.BlockSpec((8, LONG), lambda g: (0, 0)), hbm, hbm, hbm],
        out_shape=[
            jax.ShapeDtypeStruct((DI + CDIM + HEADS, PART), LOW),
            jax.ShapeDtypeStruct((OUT_PART, DM), LOW),
            jax.ShapeDtypeStruct((8, LONG), F32),
            jax.ShapeDtypeStruct((length, DM), F32),
            jax.ShapeDtypeStruct((length, DM), LOW),
            jax.ShapeDtypeStruct((LONG, DM), LOW),
        ],
        scratch_shapes=[
            pltpu.VMEM((length + EDGE, WIDE), F32),
            pltpu.VMEM((length + EDGE, WIDE), F32),
            pltpu.VMEM((NSTATE, WIDE), F32),
            pltpu.VMEM((STEPS, length, WIDE), F32),
            pltpu.VMEM((length, LONG), LOW),
            pltpu.VMEM((length // BLOCK, BLOCK, BLOCK), F32),
            pltpu.VMEM((length, 2 * NSTATE), F32),
            pltpu.VMEM((length, LANES), F32),
            pltpu.VMEM((length, LANES), F32),
            pltpu.VMEM((length, LANES), F32),
            pltpu.VMEM((length // BLOCK, 8, LANES), F32),
            pltpu.VMEM((LANES, length), F32),
            pltpu.VMEM((WIDE, DM), LOW),
            pltpu.VMEM((16, LONG), LOW),
            pltpu.VMEM((16, LONG), LOW),
            dma((3 + PARTS,)),
            pltpu.VMEM((NSTATE, DI), F32),
            pltpu.VMEM((8, DI), F32),
            pltpu.VMEM((8, DI), F32),
            pltpu.VMEM((NSTATE, DI), F32),
            pltpu.VMEM((NSTATE, DI), LOW),
            pltpu.VMEM((bits, NSTATE, DI), LOW),
            dma((bits, STEPS)),
            dma((bits, STEPS)),
            pltpu.VMEM((meets, 8, LONG), F32),
            pltpu.VMEM((meets, 8, LONG), F32),
            dma((meets,)),
            dma((meets,)),
            pltpu.VMEM((FEW, ROWS, DM), LOW),
            pltpu.VMEM((FEW, ROWS, 2 * PART), LOW),
            pltpu.VMEM((FEW, ROWS, PART), LOW),
            pltpu.VMEM((FEW, ROWS, PART), LOW),
            pltpu.VMEM((FEW, ROWS, PART), F32),
            pltpu.VMEM((SLOTS, ROWS, PART), LOW),
            dma((FEW,)),
            dma((SLOTS,)),
            dma((stages, FEW)),
            dma((stages, FEW)),
        ]
        + shares,
        compiler_params=pltpu.CompilerParams(vmem_limit_bytes=62 << 20, collective_id=2, has_side_effects=True),
        cost_estimate=pl.CostEstimate(flops=200 << 30, bytes_accessed=60 << 20, transcendentals=0),
        name="rear",
    )(proj, x, dy, bc, rb, rt, er, ew, d2, ed, dt, e2, et, states, incoming, taps, skip, heads, met, normed, tokens, upstream, gain, sums, low, dgate, wide_all, conv_all, din, grad_out, grad_gate)


def shards(tokens, norm_gain, in_weight, conv_kernel, conv_bias, step_bias, decay_log, skip_gain, out_gain, out_weight, cotangent):
    length = tokens.shape[1]
    own, upstream = tokens[0], cotangent[0]
    turned = in_weight.T
    gain = norm_gain[None]
    skip = jnp.repeat(skip_gain, HDIM)[None]
    gains = jnp.concatenate([out_gain[None], skip, jnp.zeros((6, DI), F32)], axis=0)
    skip = jnp.broadcast_to(skip, (8, DI))
    lanes = np.arange(DI) // HDIM
    e2 = jnp.asarray((np.arange(2 * LANES)[:, None] % LANES == lanes[None]).astype(LOW))
    et = jnp.asarray((lanes[:, None] == np.arange(LANES)[None]).astype(LOW))

    taps, heads, proj, normed, x, bc, dt, rb, rt, er, ew, d2, ed, state, conv_all = enter(own, gain, conv_kernel, conv_bias[None], step_bias[None], decay_log[None], e2, turned)
    incoming, met, y, states, gate, dno, wide_all = gates(normed, upstream, state, x, bc, rb, rt, er, ew, d2, e2, turned, out_weight)
    low, dy, dgate, sums, din = middle(y, bc, incoming, ed, e2, x, gate, dno, gains, length)

    def product(left, right):
        return jnp.dot(left.T, right, preferred_element_type=F32).astype(LOW)

    grad_out = product(low, upstream)
    grad_gate = product(dgate, normed[EDGE:])
    sum_in, sum_out, small, d_tokens, mixed, _ = rear(proj, x, dy, bc, rb, rt, er, ew, d2, ed, dt, e2, et, states, incoming, taps, skip, heads, met, normed, own, upstream, gain, sums, low, dgate, wide_all, conv_all, din, grad_out, grad_gate)
    return (
        mixed[None],
        d_tokens[None],
        small[5, :DM],
        sum_in.astype(F32).T,
        small[:CONV, :CDIM],
        small[CONV, :CDIM],
        small[6, DI : DI + HEADS],
        small[7, DI : DI + HEADS],
        jnp.sum(small[7, :DI].reshape(HEADS, HDIM), axis=1),
        small[6, :DI],
        sum_out.astype(F32),
    )


def solution(mesh):
    spread = P("wt", "seq", None)
    return jax.shard_map(
        shards,
        mesh=mesh,
        in_specs=(spread, P(), P("wt", None), P(), P(), P(), P(), P(), P(), P("wt", None), spread),
        out_specs=(spread, spread, P(), P("wt", None), P(), P(), P(), P(), P(), P(), P("wt", None)),
        check_vma=False,
    )
```

time: 2300 us -> 479 us (0.21); the launches traced: 2270 us -> 470 us
  waiting for transfers between devices: 1260 us -> 0 us
  local copies, waits for them, and re-layouts: 453 us -> 16.9 us
  Pallas kernels: 0 us -> 424 us
  matrix products: 303 us -> 17.6 us
  other arithmetic: 202 us -> 10.6 us
    psum x2 -> x0, waiting for transfers between devices: 575 us -> none  [the longest x1 458 us: shards(): shard_in, shard_out = lax.psum((part_in, part_out), 'seq')]
    all_gather x4 -> x0, waiting for transfers between devices: 432 us -> none  [the longest x2 285 us: prefix(): everything = jax.tree.map(lambda part: lax.all_gather(part, axis), array)]
    pallas_call x0 -> x4, Pallas kernels: none -> 424 us  [the longest x1 250 us: rear(): pl.pallas_call(rear_kernel, grid=(ALL_STEPS,), in_specs=[pl.BlockSpec((le...]
    dot_general x37 -> x2, matrix products: 303 us -> 17.6 us  [product(): return jnp.dot(left.T, right, preferred_element_type=F32).astype(LOW)]
    dynamic_update_slice x12 -> x0, local copies, waits for them, and re-layouts: 274 us -> none  [inner(): final, outputs = lax.scan(jax.checkpoint(block_step), start, pieces)]
    reduce_scatter x2 -> x0, waiting for transfers between devices: 251 us -> none  [the longest x1 251 us: shards(): lax.psum_scatter(grad_win, 'wt', scatter_dimension=0, tiled=True)]
    reduce_sum x13 -> x1, other arithmetic: 66.1 us -> 0.63 us  [shards(): jnp.sum(small[7, :DI].reshape(HEADS, HDIM), axis=1)]
    unnamed x138 -> x26, local copies, waits for them, and re-layouts: 36.8 us -> 5.29 us
  transfers between devices with their start and end apart: 10 -> 0, of which waited for: 7 -> 0; matrix products, arithmetic and copies ran while one was open for 28% -> 0% of each run, Pallas kernels for 0% -> 0%
where the time goes in v1:
time: 479 us; the launch traced here: 470 us
  Pallas kernels  424 us (89%)
  matrix products  17.6 us (4%)
  local copies, waits for them, and re-layouts  16.9 us (4%)
  other arithmetic  10.6 us (2%)
    pallas_call x1, Pallas kernels, rear(): pl.pallas_call(rear_kernel, grid=(ALL_STEPS,), in_specs=[pl.BlockSpec((le...  250 us
    pallas_call x1, Pallas kernels, gates(): pl.pallas_call(gates_kernel, in_specs=[vmem] * 11 + [hbm, hbm], out_specs...  108 us
    pallas_call x1, Pallas kernels, enter(): pl.pallas_call(enter_kernel, in_specs=[vmem] * 7 + [hbm], out_specs=[vmem...  50.9 us
    dot_general x2, matrix products, product(): return jnp.dot(left.T, right, preferred_element_type=F32).astype(LOW)  17.6 us
    pallas_call x1, Pallas kernels, middle(): pl.pallas_call(middle_kernel, grid=(length // BLOCK,), in_specs=[pl.Block...  15.6 us

profile of v1, /device:TPU:0, one launch (start us, length us, event | category | flops | bytes accessed | tf_op | source)
XLA Modules:
  0.0 470.3 jit_solution(17719105811124980248)
XLA Ops:
  0.7 0.1 pad.2.clone
  0.7 1.3 broadcast_in_dim.34.gain_ref
  2.0 1.3 broadcast_in_dim.35.bias_ref
  3.3 0.7 broadcast_in_dim.39
  4.1 0.1 broadcast_in_dim.41
  4.1 0.1 broadcast_in_dim_reshape.3
  4.2 0.8 maximum_maximum_fusion.gains_ref
  5.0 0.7 broadcast_in_dim.42.skip_ref
  5.7 50.9 %enter.1 = (f32[8,3584]{1,0:T(8,128)}, f32[8,128]{1,0:T(8,128)}, bf16[528,3376]{1,0:T(8,128)(2,1)}, bf16[528,1536]{1,0:T(8,128)(2,1)}, bf16[512,3072]{1,0:T(8,12...) custom-call(bf16[512,1536]{1,0:T(8,128)(2,1)} %bitcast.25, ...), custom_call_target="tpu_custom_call" | custom-call | flops 42949672960 | bytes 31457280 | tf_op jit(solution)/shard_map/enter/pallas_call | solution.py:421
  56.6 0.0 copy-start
  56.6 0.0 copy-start.3
  56.6 0.0 copy-start.4
  56.6 108.0 %gates.1 = (bf16[128,3072]{1,0:T(8,128)(2,1)}, f32[8,3072]{1,0:T(8,128)}, f32[512,3072]{1,0:T(8,128)}, bf16[4,128,3072]{2,1,0:T(8,128)(2,1)}, bf16[512,3072]{1,0...) custom-call(bf16[528,1536]{1,0:T(8,128)(2,1)} %get-tuple-element.45.normed_ref, ...), custom_call_target="tpu_custom_call" | custom-call | flops 53687091200 | bytes 52428800 | tf_op jit(solution)/shard_map/gates/pallas_call | solution.py:570
  164.6 0.0 copy-done
  164.6 0.0 copy-done.3
  164.6 0.0 copy-done.4
  164.6 0.0 copy-start.2
  164.6 1.1 copy-done.2
  165.7 0.0 copy-start.9
  165.7 15.6 %middle.1 = (bf16[512,3072]{1,0:T(8,128)(2,1)}, bf16[512,3072]{1,0:T(8,128)(2,1)}, bf16[512,3072]{1,0:T(8,128)(2,1)}, f32[8,3072]{1,0:T(8,128)S(1)}, f32[128,3072]{1,0:T(8,128)S(1)}) custom-call(f32[512,3072]{1,0:T(8,128)} %get-tuple-element.53.y_ref, bf16[512,256]{1,0:T(8,128)(2,1)S(1)} %copy-done.3, bf16[128,3072]{1,0:T(8,128)(2,1)S(1)} %copy-done.2, ...), custom_call_target="tpu_custom_call" | custom-call | flops 12884901888 | bytes 33554432 | tf_op jit(solution)/shard_map/middle/pallas_call | solution.py:241
  181.4 0.0 copy-start.1
  181.4 0.0 copy-start.5
  181.4 0.0 copy-done.9
  181.4 0.0 copy-start.10
  181.4 0.0 copy-start.11
  181.4 10.1 %convolution_convert_fusion.1.gout_ref = bf16[3072,1536]{1,0:T(8,128)(2,1)} fusion(bf16[512,3072]{1,0:T(8,128)(2,1)} %get-tuple-element.65.low_ref, bf16[1,512,1536]{2,1,0:T(8,128)(2,1)S(1)} %copy-done.9), kind=kOutput, calls=%fused_computation.1 | convolution fusion | flops 4836556800 | bytes 14155776 | tf_op jit(solution)/shard_map/dot_general | solution.py:1230
  191.5 0.0 copy-done.1
  191.5 0.0 copy-done.5
  191.5 0.0 copy-done.10
  191.5 0.0 copy-done.11
  191.5 7.6 %convolution_convert_fusion.ggate_ref = bf16[3072,1536]{1,0:T(8,128)(2,1)} fusion(bf16[512,3072]{1,0:T(8,128)(2,1)S(1)} %copy-done.10, bf16[528,1536]{1,0:T(8,128)(2,1)S(1)} %copy-done.11), kind=kOutput, calls=%fused_computation | convolution fusion | flops 4836556800 | bytes 14155776 | tf_op jit(solution)/shard_map/dot_general | solution.py:1230
  199.1 249.6 %rear.1 = (bf16[6448,384]{1,0:T(8,128)(2,1)}, bf16[768,1536]{1,0:T(8,128)(2,1)}, f32[8,3584]{1,0:T(8,128)}, f32[512,1536]{1,0:T(8,128)}, bf16[512,1536]{1,0:T(8,128)(2,1)}, /*index=5*/bf16[3584,1536]{1,0:T(8,128)(2,1)}) custom-call(bf16[528,3376]{1,0:T(8,128)(2,1)} %get-tuple-element.43.pc_ref, bf16[512,3072]{1,0:T(8,128)(2,1)} %get-tuple-element.44.x_ref, ...), custom_call_target="tpu_custom_call" | custom-call | flops 214748364800 | bytes 62914560 | tf_op jit(solution)/shard_map/rear/pallas_call | solution.py:1121
  448.7 1.3 slice_bitcast_fusion
  450.0 1.4 slice_reduce_fusion.2
  451.4 1.5 slice_reduce_fusion
  452.9 1.6 fusion.2
  454.5 1.5 slice.26
  456.1 0.1 reshape_squeeze.3
  456.1 0.6 reduce_sum.9
  456.8 0.0 copy-start.6
  456.8 4.6 convert_element_type.12
  461.4 0.0 copy-done.6
  461.4 0.0 copy-start.8
  461.4 4.5 convert_bitcast_fusion
  465.9 0.0 copy-done.8
  465.9 0.0 copy-start.7
  465.9 1.1 copy.26
  467.1 1.3 copy-done.7
  468.4 1.7 copy.27
  (1 shorter events, 0.0 us)
Async XLA Ops:
  56.6 108.0 %copy-start = (bf16[256,3072]{1,0:T(8,128)(2,1)S(1)}, bf16[256,3072]{1,0:T(8,128)(2,1)}, u32[]{:S(2)}) copy-start(bf16[256,3072]{1,0:T(8,128)(2,1)} %constant.2.clone.e2_ref) | copy-start | bytes 4718596
  56.6 108.0 %copy-start.3 = (bf16[512,256]{1,0:T(8,128)(2,1)S(1)}, bf16[512,256]{1,0:T(8,128)(2,1)}, u32[]{:S(2)}) copy-start(bf16[512,256]{1,0:T(8,128)(2,1)} %get-tuple-element.47.bc_ref) | copy-start | bytes 786436
  56.6 108.0 %copy-start.4 = (bf16[512,256]{1,0:T(8,128)(2,1)S(1)}, bf16[512,256]{1,0:T(8,128)(2,1)}, u32[]{:S(2)}) copy-start(bf16[512,256]{1,0:T(8,128)(2,1)} %get-tuple-element.55.ed_ref) | copy-start | bytes 786436
  164.6 1.1 copy-start.2
  165.7 15.6 %copy-start.9 = (bf16[1,512,1536]{2,1,0:T(8,128)(2,1)S(1)}, bf16[1,512,1536]{2,1,0:T(8,128)(2,1)}, u32[]{:S(2)}) copy-start(bf16[1,512,1536]{2,1,0:T(8,128)(2,1)} %param.23) | copy-start | bytes 4718596
  181.4 10.1 %copy-start.1 = (f32[128,3072]{1,0:T(8,128)}, f32[128,3072]{1,0:T(8,128)S(1)}, u32[]{:S(2)}) copy-start(f32[128,3072]{1,0:T(8,128)S(1)} %get-tuple-element.69.din_ref) | copy-start | bytes 4718596
  181.4 10.1 %copy-start.5 = (f32[8,3072]{1,0:T(8,128)}, f32[8,3072]{1,0:T(8,128)S(1)}, u32[]{:S(2)}) copy-start(f32[8,3072]{1,0:T(8,128)S(1)} %get-tuple-element.64.sums_ref) | copy-start | bytes 294916
  181.4 10.1 %copy-start.10 = (bf16[512,3072]{1,0:T(8,128)(2,1)S(1)}, bf16[512,3072]{1,0:T(8,128)(2,1)}, u32[]{:S(2)}) copy-start(bf16[512,3072]{1,0:T(8,128)(2,1)} %get-tuple-element.66.dgate_ref) | copy-start | bytes 9437188
  181.4 10.1 %copy-start.11 = (bf16[528,1536]{1,0:T(8,128)(2,1)S(1)}, bf16[528,1536]{1,0:T(8,128)(2,1)}, u32[]{:S(2)}) copy-start(bf16[528,1536]{1,0:T(8,128)(2,1)} %get-tuple-element.45.normed_ref) | copy-start | bytes 4866052
  456.8 4.7 copy-start.6
  461.4 4.5 copy-start.8
  465.9 2.5 copy-start.7
